TPU v7x, 32 devices: a whole 2x2x4 slice. The times are simulated.
32 devices in a mesh: blk: 16 (over z, y, x), tp: 2 (over core).
Axes of the slice: x: 2, y: 2, z: 4, core: 2. Of those that a mesh axis runs over, the one named last changes fastest.
Arguments:
- q_tokens: int32 [64, 64], P('blk'), may hold values from 0 to 30521
- p_tokens: int32 [128, 256], P('blk'), may hold values from 0 to 30521
- q_lengths: int32 [64], P('blk'), may hold values from 8 to 64, as said below
- p_lengths: int32 [128], P('blk'), may hold values from 64 to 256, as said below
- positive: int32 [64], P('blk'), may hold values from -1 to 127, as said below
- table: float32 [31104, 768], P('blk', 'tp'), may hold values from -6 to 6
- table_moment: float32 [31104, 768], P('blk', 'tp')
- table_second: float32 [31104, 768], P('blk', 'tp'), as said below
- blocks: float32 [2, 192, 192, 192], P('tp', 'blk')
- left_stats: float32 [2, 192, 192, 192], P('tp', 'blk'), as said below
- right_stats: float32 [2, 192, 192, 192], P('tp', 'blk'), as said below
- left_roots: float32 [2, 192, 192, 192], P('tp', 'blk'), as said below
- right_roots: float32 [2, 192, 192, 192], P('tp', 'blk'), as said below
- vectors: float32 [2, 2, 2304], P('tp', None, 'blk'), may hold values from -1.8 to 1.8
- vector_moment: float32 [2, 2, 2304], P('tp', None, 'blk')
- vector_second: float32 [2, 2, 2304], P('tp', None, 'blk'), as said below
- shared: float32 [14, 768], P(None, 'blk')
- shared_moment: float32 [14, 768], P(None, 'blk')
- shared_second: float32 [14, 768], P(None, 'blk'), as said below
Outputs:
- loss_sum: float32 [], replicated
- positives_count: float32 [], replicated
- grad_norm: float32 [], replicated
- block_grads: float32 [2, 192, 192, 192], P('tp', 'blk')
- left_new: float32 [2, 192, 192, 192], P('tp', 'blk')
- right_new: float32 [2, 192, 192, 192], P('tp', 'blk')
- blocks_new: float32 [2, 192, 192, 192], P('tp', 'blk')
- table_moment_new: float32 [31104, 768], P('blk', 'tp')
- table_second_new: float32 [31104, 768], P('blk', 'tp')
- table_new: float32 [31104, 768], P('blk', 'tp')
- vector_moment_new: float32 [2, 2, 2304], P('tp', None, 'blk')
- vector_second_new: float32 [2, 2, 2304], P('tp', None, 'blk')
- vectors_new: float32 [2, 2, 2304], P('tp', None, 'blk')
- shared_moment_new: float32 [14, 768], P(None, 'blk')
- shared_second_new: float32 [14, 768], P(None, 'blk')
- shared_new: float32 [14, 768], P(None, 'blk')
Inputs may be any that keep to these rules, and one draw needn't show every extreme that they name: `q_lengths`: one question in every draw has length 64. `p_lengths`: one passage in every draw has length 256. -1 means that the question has no positive; the last question of every aligned 4 has one. `left_stats`: symmetric. `right_stats`: symmetric. `left_roots`: symmetric. `right_roots`: symmetric. `table_second`: positive. `vector_second`: positive. `shared_second`: positive.
All inputs are finite; a program needn't handle non-finite values.
Results may differ from a plain program's by a relative error of at most 0.017.
The roundings to bfloat16 on the way count: a program that leaves them out, or rounds other values in their place, can miss the bound.
Values may be sent and summed in bfloat16 or wider, within the bound.
No kernel may reach another device: no remote copies, remote signals or barrier semaphores. Data moves between devices by JAX's collectives and lax.ppermute only.
A program may use at most 320 MiB of HBM per device.

v0:
```python
from functools import partial

import jax
import jax.numpy as jnp
from jax import lax
from jax.experimental import pallas as pl
from jax.experimental.pallas import tpu as pltpu
from jax.sharding import PartitionSpec as P

bf16, f32 = jnp.bfloat16, jnp.float32
MODEL_WIDTH = 768
HALF = MODEL_WIDTH // 2
HD = 64
FF = 3072
UNITS = FF // 2
NORM_EPS = 1e-06
VMEM_LIMIT = 60 * 1024 * 1024
LAYERS = 2
STEP = 10
VOCAB = 30522
CLIP = 0.05
BETA_ONE = 0.9
BETA_TWO = 0.999
STAT_DECAY = 0.95
ADAM_RATE = 0.5
SHAMPOO_RATE = 0.5
WEIGHT_DECAY = 0.01
ADAM_EPS = 1e-08
PRECISION_MAX = lax.Precision.HIGHEST
GROUP = 2
SLOTS = 92
LANES = 128

TAIL = (
    0.16918798443114483,
    0.17071555704933744,
    0.14833696008811015,
    0.2149342153930891,
    -0.09466890560267835,
    0.5477451349382827,
    -0.5122991151213244,
    0.4855729957946344,
    -0.12952484655737367,
)


def gelu_parts(u):
    t = 1.0 / (1.0 + (0.3 * 0.5**0.5) * jnp.abs(u))
    poly = jnp.full_like(t, TAIL[-1])
    for term in TAIL[-2::-1]:
        poly = poly * t + term
    bell = jnp.exp(u * u * -0.5)
    tail = (0.5 * t) * poly * bell
    below = jnp.where(u >= 0, 1.0 - tail, tail)
    return u * below, below + u * (bell * 0.3989422804014327)


def dot(a, b, contract=((1,), (0,))):
    return lax.dot_general(a, b, (contract, ((), ())), preferred_element_type=f32)


NT = ((1,), (1,))
TN = ((0,), (0,))


def unit(value):
    centred = value - jnp.mean(value, axis=-1, keepdims=True)
    rate = lax.rsqrt(jnp.mean(centred * centred, axis=-1, keepdims=True) + NORM_EPS)
    return centred * rate, rate


def unit_back(grad, hat, rate):
    return rate * (
        grad
        - jnp.mean(grad, axis=-1, keepdims=True)
        - hat * jnp.mean(grad * hat, axis=-1, keepdims=True)
    )


def total(value):
    return jnp.sum(value, axis=0, keepdims=True)


def row_lengths(lengths, rows, axis, seg, shape):
    index = lax.broadcasted_iota(jnp.int32, shape, axis)
    if seg == rows:
        return index, None, lengths[pl.program_id(0)]
    which = index // seg
    length = jnp.zeros(shape, jnp.int32)
    before = pl.program_id(0) * (rows // seg)
    for place in range(rows // seg):
        length = jnp.where(which == place, lengths[before + place], length)
    return index - which * seg, which, length


def row_live(lengths, rows, seg):
    place, _, length = row_lengths(lengths, rows, 0, seg, (rows, 1))
    return (place < length).astype(f32), length


def key_mask(lengths, rows, seg):
    if seg == rows:
        place, _, length = row_lengths(lengths, rows, 1, seg, (1, rows))
        return place < length
    place, which, length = row_lengths(lengths, rows, 1, seg, (rows, rows))
    mine = lax.broadcasted_iota(jnp.int32, (rows, rows), 0) // seg
    return (which == mine) & (place < length)


def key_mask_across(lengths, rows, seg):
    place, which, length = row_lengths(lengths, rows, 0, seg, (rows, 1))
    if seg == rows:
        return place < length
    mine = lax.broadcasted_iota(jnp.int32, (rows, rows), 1) // seg
    return (which == mine) & (place < length)


def load_weights(groups, order, first, spot, mats, sem):
    side, wide = groups[0].shape[1:]
    starts, waits, at = [], [], 0
    for mat in mats:
        for row in range(mat.shape[0] // side):
            for column in range(mat.shape[1] // wide):
                to = mat.at[row * side : (row + 1) * side, column * wide : (column + 1) * wide]
                if len(groups) == 1:
                    choices = [(None, groups[0].at[order[first + at]])]
                else:
                    choices = group_choices(groups, order, first + at, spot)
                copies = [
                    (where, pltpu.make_async_copy(part, to, sem.at[at])) for where, part in choices
                ]
                starts += copies
                waits.append(copies[0][1])
                at += 1
    for where, copy in starts:
        if where is None:
            copy.start()
        else:
            pl.when(where)(copy.start)
    for copy in waits:
        copy.wait()


def group_choices(groups, layer, group, spot):
    owner, place = divmod(group, 6)
    plane, own_y, own_x = owner // 4, owner // 2 % 2, owner % 2
    is_first = spot[2 + layer] == (0 if plane == 1 - layer else 1)
    far_x, far_y = spot[0] != own_x, spot[1] != own_y
    near_x, near_y = jnp.logical_not(far_x), jnp.logical_not(far_y)
    part, rest = divmod(place, 3)
    choices = []
    for here, (own, by_x, by_y, *both) in (
        (is_first, groups[:5]),
        (jnp.logical_not(is_first), groups[5:]),
    ):
        choices += [
            (here & near_x & near_y, own.at[place]),
            (here & far_x & near_y, by_x.at[place]),
            (here & near_x & far_y, by_y.at[place]),
            (here & far_x & far_y, both[part].at[rest]),
        ]
    return choices


def gather_near(links, piece):
    return links.over_x(piece), links.over_y(piece)


def gather_far(links, by_x, by_y):
    half = by_x.shape[0] // 2
    return links.over_y(by_x[:half]), links.over_x(by_y[half:])


def store_groups(mats, lows, grads, sem):
    side, wide = grads.shape[1:]
    copies, at = [], 0
    for mat, low in zip(mats, lows):
        low[...] = mat[...].astype(bf16)
        for row in range(mat.shape[0] // side):
            for column in range(mat.shape[1] // wide):
                part = low.at[row * side : (row + 1) * side, column * wide : (column + 1) * wide]
                copies.append(pltpu.make_async_copy(part, grads.at[at], sem.at[at]))
                at += 1
    for copy in copies:
        copy.start()
    for copy in copies:
        copy.wait()


def store_planes(first, mats, lows, spot, sets, sem):
    side, wide = sets[0][1].shape[-2:]
    count = 3
    copies, at = [], 0
    for mat, low in zip(mats, lows):
        low[...] = mat[...].astype(bf16)
        for row in range(mat.shape[0] // side):
            for column in range(mat.shape[1] // wide):
                owner, place = divmod(first + at, 2 * count)
                plane, own_y, own_x = owner // 4, owner // 2 % 2, owner % 2
                planes, *refs = next(item for item in sets if plane in item[0])
                plane = planes.index(plane)
                by_y = place < count
                mine = spot[1] == own_y if by_y else spot[0] == own_x
                index = (plane * 2 + (own_x if by_y else own_y)) * count + place % count
                send, keep = (refs[0], refs[2]) if by_y else (refs[1], refs[3])
                region = (
                    slice(row * side, (row + 1) * side),
                    slice(column * wide, (column + 1) * wide),
                )
                copies.append(
                    (mine, pltpu.make_async_copy(mat.at[region], keep.at[index], sem.at[at]))
                )
                copies.append(
                    (
                        jnp.logical_not(mine),
                        pltpu.make_async_copy(low.at[region], send.at[index], sem.at[at]),
                    )
                )
                at += 1
    for where, copy in copies:
        pl.when(where)(copy.start)
    for where, copy in copies:
        pl.when(where)(copy.wait)


def head_lanes(rows):
    return lax.broadcasted_iota(jnp.int32, (rows, 2 * HD), 1) < HD


def embedded(seg, spot, mine, theirs, place_mine, place_theirs):
    rows = mine.shape[0]

    def side_of(ref, places):
        place = jnp.concatenate([places[:seg].astype(f32)] * (rows // seg), axis=0)
        return ref[...].astype(f32) + place

    own, other = side_of(mine, place_mine), side_of(theirs, place_theirs)
    first = spot[4] == 0
    return jnp.concatenate([jnp.where(first, own, other), jnp.where(first, other, own)], axis=1)


def attention_forward_body(
    seg, order, lengths, spot, mine, theirs, place_mine, place_theirs, bias, params, *rest,
):
    groups, rest = rest[:-8], rest[-8:]
    state, qkv, context, logs, out, joint, output_weight, sem = rest
    rows = mine.shape[0]

    @pl.when(pl.program_id(0) == 0)
    def _():
        load_weights(groups, order, 0, spot, (joint, output_weight), sem)

    hat, _ = unit(embedded(seg, spot, mine, theirs, place_mine, place_theirs))
    value = hat * params[0:1] + params[1:2]
    state[...] = value
    projected = dot(value.astype(bf16), joint[...])
    shift = jnp.concatenate(
        [bias[:, :HALF], jnp.zeros((1, HALF), f32), bias[:, HALF : 2 * HALF]], axis=1
    )
    projected = (projected + shift).astype(bf16)
    qkv[...] = projected
    mask = key_mask(lengths, rows, seg)
    first = head_lanes(rows)
    contexts = []
    for pair in range(HALF // (2 * HD)):
        lanes = slice(pair * 2 * HD, (pair + 1) * 2 * HD)
        query = projected[:, :HALF][:, lanes] * jnp.asarray(HD**-0.5, bf16)
        key = projected[:, HALF : 2 * HALF][:, lanes]
        what = projected[:, 2 * HALF :][:, lanes]
        sides = []
        for head in range(2):
            only = jnp.where(first if head == 0 else ~first, query, jnp.zeros_like(query))
            scores = jnp.where(mask, dot(only, key, NT), -1e30)
            top = jnp.max(scores, axis=-1, keepdims=True)
            expo = jnp.exp(scores - top)
            size = jnp.sum(expo, axis=-1, keepdims=True)
            logs[:, 2 * pair + head : 2 * pair + head + 1] = top + jnp.log(size)
            sides.append(dot((expo * (1.0 / size)).astype(bf16), what))
        contexts.append(jnp.where(first, sides[0], sides[1]))
    contexts = jnp.concatenate(contexts, axis=1).astype(bf16)
    context[...] = contexts
    out[...] = dot(contexts, output_weight[...]).astype(bf16)


def forward_ffn_body(
    order, spot, state, own, other, bias, params, *rest,
):
    groups, rest = rest[:-7], rest[-7:]
    hidden, active, slope, out, up_weight, down_weight, sem = rest
    wide = groups[0].shape[2]

    @pl.when(pl.program_id(0) == 0)
    def _():
        load_weights(groups, order, ATTENTION_GROUPS, spot, (up_weight, down_weight), sem)

    hat, _ = unit(state[...] + (own[...].astype(f32) + other[...].astype(f32)) + params[0:1])
    value = hat * params[1:2] + params[2:3]
    hidden[...] = value
    low = value.astype(bf16)
    step = 2 * wide if UNITS % (2 * wide) == 0 else wide
    result = jnp.zeros(out.shape, f32)
    for start in range(0, UNITS, step):
        columns = slice(start, start + step)
        up = dot(low, up_weight[:, columns]) + bias[:, 2 * HALF + start : 2 * HALF + start + step]
        act, rise = gelu_parts(up)
        act = act.astype(bf16)
        active[:, columns] = act
        slope[:, columns] = rise.astype(bf16)
        result = result + dot(act, down_weight[columns, :])
    out[...] = result.astype(bf16)


def pool_body(seg, lengths, hidden, own, other, params, out):
    rows = hidden.shape[0]
    hat, _ = unit(hidden[...] + (own[...].astype(f32) + other[...].astype(f32)) + params[3:4])
    output = hat * params[4:5] + params[5:6]
    live, _ = row_live(lengths, rows, seg)
    output = output * live
    for place in range(rows // seg):
        index = pl.program_id(0) * (rows // seg) + place
        mean = total(output[place * seg : (place + 1) * seg]) / lengths[index].astype(f32)
        out[pl.ds(index, 1), :] = mean


def ffn_backward_body(
    seg, order, sets, amount, lengths, spot, d_pooled, hidden, own, other, active, slope, params,
    *rest,
):
    groups, rest = rest[:amount], rest[amount:]
    base, out, sums, d_bias, *rest = rest
    grads, (up_weight, down_weight, d_up, d_down, sem) = tuple(rest[:-5]), rest[-5:]
    rows = hidden.shape[0]
    wide = groups[0].shape[2]
    step_at, last = pl.program_id(0), pl.num_programs(0) - 1

    @pl.when(step_at == 0)
    def _():
        load_weights(groups, order, ATTENTION_GROUPS, spot, (up_weight, down_weight), sem)
        d_up[...] = jnp.zeros_like(d_up)
        d_down[...] = jnp.zeros_like(d_down)
        sums[...] = jnp.zeros_like(sums)
        d_bias[...] = jnp.zeros_like(d_bias)

    live, length = row_live(lengths, rows, seg)
    pooled = jnp.concatenate(
        [
            jnp.broadcast_to(
                d_pooled[pl.ds(step_at * (rows // seg) + place, 1), :], (seg, MODEL_WIDTH)
            )
            for place in range(rows // seg)
        ],
        axis=0,
    )
    d_output = pooled / length.astype(f32) * live
    value = hidden[...]
    hat, rate = unit(value + (own[...].astype(f32) + other[...].astype(f32)) + params[3:4])
    d_sum = unit_back(d_output * params[4:5], hat, rate)
    base[...] = d_sum
    sums[0:1, :] += total(d_sum)
    sums[1:2, :] += total(d_output * hat)
    sums[2:3, :] += total(d_output)
    low = d_sum.astype(bf16)
    hidden_low = value.astype(bf16)
    step = 2 * wide if UNITS % (2 * wide) == 0 else wide
    result = jnp.zeros(out.shape, f32)
    for start in range(0, UNITS, step):
        columns = slice(start, start + step)
        d_down[columns, :] += dot(active[:, columns], low, TN)
        d_act = dot(low, down_weight[columns, :], NT)
        d_pre = (d_act * slope[:, columns].astype(f32)).astype(bf16)
        d_bias[:, columns] += total(d_pre.astype(f32))
        d_up[:, columns] += dot(hidden_low, d_pre, TN)
        result = result + dot(d_pre, up_weight[:, columns], NT)
    out[...] = result.astype(bf16)

    @pl.when(step_at == last)
    def _():
        mats, lows = (d_up, d_down), (up_weight, down_weight)
        if sets is None:
            store_groups(mats, lows, grads[0], sem)
        else:
            to = [(planes,) + grads[4 * at : 4 * at + 4] for at, planes in enumerate(sets)]
            store_planes(ATTENTION_GROUPS, mats, lows, spot, to, sem)


def attention_backward_body(
    seg, order, planes, carry_in, carry_out, amount, lengths, spot, carried, back_own, back_other,
    state, own, other, qkv, context, logs, params, *rest,
):
    groups, rest = rest[:amount], rest[amount:]
    joint, output_weight, d_joint, d_output_weight, sem = rest[-5:]
    carry, rest = (rest[:4], rest[4:-5]) if carry_in else (None, rest[:-5])
    if planes is not None and not carry_out:
        rest = rest[4:]
    base, out, sums, d_bias, *results = rest
    rows = state.shape[0]
    step_at, last = pl.program_id(0), pl.num_programs(0) - 1

    @pl.when(step_at == 0)
    def _():
        load_weights(groups, order, 0, spot, (joint, output_weight), sem)
        if carry is None:
            d_joint[...] = jnp.zeros_like(d_joint)
            d_output_weight[...] = jnp.zeros_like(d_output_weight)
            sums[...] = jnp.zeros_like(sums)
            d_bias[...] = jnp.zeros_like(d_bias)
        else:
            copies = [
                pltpu.make_async_copy(carry[0], d_joint, sem.at[0]),
                pltpu.make_async_copy(carry[1], d_output_weight, sem.at[1]),
            ]
            for copy in copies:
                copy.start()
            for copy in copies:
                copy.wait()
            sums[...] = carry[2][...]
            d_bias[...] = carry[3][...]

    d_hidden = carried[...] + (back_own[...].astype(f32) + back_other[...].astype(f32))
    value = state[...]
    hat, rate = unit(value + (own[...].astype(f32) + other[...].astype(f32)) + params[0:1])
    d_sum = unit_back(d_hidden * params[1:2], hat, rate)
    base[...] = d_sum
    sums[0:1, :] += total(d_sum)
    sums[1:2, :] += total(d_hidden * hat)
    sums[2:3, :] += total(d_hidden)
    low = d_sum.astype(bf16)
    d_output_weight[...] += dot(context[...], low, TN)
    d_context = dot(low, output_weight[...], NT).astype(bf16)
    mask = key_mask_across(lengths, rows, seg)
    logs_across = jnp.transpose(logs[...])
    first = head_lanes(rows)
    d_queries, d_keys, d_values = [], [], []
    for pair in range(HALF // (2 * HD)):
        lanes = slice(pair * 2 * HD, (pair + 1) * 2 * HD)
        query = qkv[:, pair * 2 * HD : (pair + 1) * 2 * HD] * jnp.asarray(HD**-0.5, bf16)
        key = qkv[:, HALF + pair * 2 * HD : HALF + (pair + 1) * 2 * HD]
        what = qkv[:, 2 * HALF + pair * 2 * HD : 2 * HALF + (pair + 1) * 2 * HD]
        d_pair = d_context[:, lanes]
        sides = []
        for head in range(2):
            mine = first if head == 0 else ~first
            only = jnp.where(mine, query, jnp.zeros_like(query))
            d_only = jnp.where(mine, d_pair, jnp.zeros_like(d_pair))
            scores = jnp.where(mask, dot(key, only, NT), -1e30)
            weights = jnp.exp(scores - logs_across[2 * pair + head : 2 * pair + head + 1, :])
            spread = weights * dot(what, d_only, NT)
            d_scores = spread - weights * total(spread)
            d_scores = d_scores.astype(bf16)
            sides.append(
                (
                    dot(d_scores, key, TN),
                    dot(d_scores, query),
                    dot(weights.astype(bf16), d_pair),
                )
            )
        d_queries.append(jnp.where(first, sides[0][0], sides[1][0]) * HD**-0.5)
        d_keys.append(jnp.where(first, sides[0][1], sides[1][1]))
        d_values.append(jnp.where(first, sides[0][2], sides[1][2]))
    d_qkv = jnp.concatenate(d_queries + d_keys + d_values, axis=1).astype(bf16)
    d_bias[...] += total(d_qkv.astype(f32))
    d_joint[...] += dot(value.astype(bf16), d_qkv, TN)
    out[...] = dot(d_qkv, joint[...], NT).astype(bf16)

    @pl.when(step_at == last)
    def _():
        mats, lows = (d_joint, d_output_weight), (joint, output_weight)
        if carry_out:
            copies = [
                pltpu.make_async_copy(d_joint, results[0], sem.at[0]),
                pltpu.make_async_copy(d_output_weight, results[1], sem.at[1]),
            ]
            for copy in copies:
                copy.start()
            for copy in copies:
                copy.wait()
        elif planes is None:
            store_groups(mats, lows, results[0], sem)
        else:
            store_planes(0, mats, lows, spot, [(planes,) + tuple(results)], sem)


def expand_body(slots, fetched, out):
    hot = lax.broadcasted_iota(jnp.int32, (out.shape[0], fetched.shape[0]), 1) == slots[...]
    out[...] = dot(hot.astype(bf16), fetched[...]).astype(bf16)


def embed_backward_body(
    segs, starts, parts, *refs
):
    sources = [refs[at * 3 : at * 3 + 3] for at in range(len(starts))]
    smalls = refs[3 * len(starts) : 3 * len(starts) + 8]
    mine, theirs, place_mine, place_theirs, slots, spot, params, out, sums = refs[-11:-2]
    d_place, picked = refs[-2:]
    rows = mine.shape[0]
    step_at = pl.program_id(0)

    @pl.when(step_at == 0)
    def _():
        picked[...] = jnp.zeros_like(picked)
        d_place[...] = jnp.zeros_like(d_place)
        sums[...] = jnp.zeros_like(sums)

    def work(seg, base, own, other):
        d_state = base[...] + (own[...].astype(f32) + other[...].astype(f32))
        hat, rate = unit(embedded(seg, spot, mine, theirs, place_mine, place_theirs))
        d_rows = unit_back(d_state * params[0:1], hat, rate)
        sums[0:1, :] += total(d_state * hat)
        sums[1:2, :] += total(d_state)
        own = jnp.where(spot[4] == 0, d_rows[:, :HALF], d_rows[:, HALF:])
        for place in range(rows // seg):
            d_place[:seg, :] += own[place * seg : (place + 1) * seg]
        hot = lax.broadcasted_iota(jnp.int32, (out.shape[0], rows), 0) == slots[0]
        hot = hot.astype(bf16)
        high = own.astype(bf16)
        low = (own - high.astype(f32)).astype(bf16)
        picked[...] += dot(hot, high) + dot(hot, low)

    ends = starts[1:] + (None,)
    for source, seg, start, end in zip(sources, segs, starts, ends):
        here = step_at >= start
        if end is not None:
            here = here & (step_at < end)

        @pl.when(here)
        def _():
            work(seg, *source)

    @pl.when(step_at == pl.num_programs(0) - 1)
    def _():
        width, share = out.shape[0] // parts, rows // parts
        for part in range(parts):
            at = part * width + SLOTS
            picked[at : at + share, :] = d_place[part * share : (part + 1) * share, :]
        lines = []
        for bias, up_bias in (smalls[0:2], smalls[2:4]):
            lines += [bias[:, :HALF], bias[:, 2 * HALF :]]
            lines += [up_bias[:, at : at + HALF] for at in range(0, UNITS, HALF)]
        for at in (0, HALF):
            lines += [sums[row : row + 1, at : at + HALF] for row in range(2)]
            lines += [
                value[row : row + 1, at : at + HALF] for value in smalls[4:] for row in range(3)
            ]
        per = -(-len(lines) // parts)
        for line, value in enumerate(lines):
            at = line // per * width + SLOTS + share + line % per
            picked[at : at + 1, :] = value
        out[...] = picked[...].astype(bf16)


def whole(shape):
    return pl.BlockSpec(shape, lambda i: (0,) * len(shape), pipeline_mode=pl.Buffered(1))


def by_rows(rows, width, offset=0):
    return pl.BlockSpec((rows, width), lambda i: (i + offset, 0))


SMEM = pl.BlockSpec(memory_space=pltpu.SMEM)


def fixed(shape):
    return pl.BlockSpec(shape, lambda i: (0,) * len(shape))


def call(body, grid, in_specs, out_specs, out_shape, scratch=(), us=1.0, name=None, alias=None):
    return pl.pallas_call(
        body,
        grid=(grid,),
        in_specs=in_specs,
        out_specs=out_specs,
        out_shape=[jax.ShapeDtypeStruct(*item) for item in out_shape],
        scratch_shapes=list(scratch),
        compiler_params=pltpu.CompilerParams(vmem_limit_bytes=VMEM_LIMIT),
        cost_estimate=pl.CostEstimate(
            flops=int(us * 1.15e8), bytes_accessed=int(us * 1e4), transcendentals=0
        ),
        input_output_aliases=alias or {},
        name=name,
    )


ANY = pl.BlockSpec(memory_space=pl.ANY)
ATTENTION_GROUPS = 16
FFN_GROUPS = 32


def attention_forward(
    layer, seg, rows, blocks, first, lengths, spot, mine, theirs, groups, order, bias, params
):
    place = mine.shape[0] // rows - 1
    at_place = pl.BlockSpec((rows, HALF), lambda i: (place, 0), pipeline_mode=pl.Buffered(1))
    count = blocks * rows
    return call(
        partial(attention_forward_body, seg, order),
        blocks,
        [
            SMEM,
            SMEM,
            by_rows(rows, HALF, first),
            by_rows(rows, HALF, first),
            at_place,
            at_place,
            whole(bias.shape),
            whole(params.shape),
        ]
        + [ANY] * len(groups),
        [
            by_rows(rows, MODEL_WIDTH),
            by_rows(rows, 3 * HALF),
            by_rows(rows, HALF),
            by_rows(rows, 2 * HD),
            by_rows(rows, MODEL_WIDTH),
        ],
        [
            ((count, MODEL_WIDTH), f32),
            ((count, 3 * HALF), bf16),
            ((count, HALF), bf16),
            ((count, 2 * HD), f32),
            ((count, MODEL_WIDTH), bf16),
        ],
        [
            pltpu.VMEM((MODEL_WIDTH, 3 * HALF), bf16),
            pltpu.VMEM((HALF, MODEL_WIDTH), bf16),
            pltpu.SemaphoreType.DMA((ATTENTION_GROUPS,)),
        ],
        us=2.5 * blocks,
        name=f"attention_forward_{layer}",
    )(lengths, spot, mine, theirs, mine, theirs, bias, params, *groups)


def ffn_forward(layer, rows, spot, state, own, other, groups, order, bias, params):
    count = state.shape[0]
    return call(
        partial(forward_ffn_body, order),
        count // rows,
        [
            SMEM,
            by_rows(rows, MODEL_WIDTH),
            by_rows(rows, MODEL_WIDTH),
            by_rows(rows, MODEL_WIDTH),
            whole(bias.shape),
            whole(params.shape),
        ]
        + [ANY] * len(groups),
        [
            by_rows(rows, MODEL_WIDTH),
            by_rows(rows, UNITS),
            by_rows(rows, UNITS),
            by_rows(rows, MODEL_WIDTH),
        ],
        [
            ((count, MODEL_WIDTH), f32),
            ((count, UNITS), bf16),
            ((count, UNITS), bf16),
            ((count, MODEL_WIDTH), bf16),
        ],
        [
            pltpu.VMEM((MODEL_WIDTH, UNITS), bf16),
            pltpu.VMEM((UNITS, MODEL_WIDTH), bf16),
            pltpu.SemaphoreType.DMA((FFN_GROUPS,)),
        ],
        us=3.8 * count / 256,
        name=f"ffn_forward_{layer}",
    )(spot, state, own, other, bias, params, *groups)


def pool_forward(layer, seg, rows, lengths, hidden, own, other, params):
    count = hidden.shape[0]
    return call(
        partial(pool_body, seg),
        count // rows,
        [
            SMEM,
            by_rows(rows, MODEL_WIDTH),
            by_rows(rows, MODEL_WIDTH),
            by_rows(rows, MODEL_WIDTH),
            whole(params.shape),
        ],
        [fixed((count // seg, MODEL_WIDTH))],
        [((count // seg, MODEL_WIDTH), f32)],
        us=1.1 * (count // rows),
        name=f"pool_{layer}",
    )(lengths, hidden, own, other, params)[0]


def plane_shapes(planes, side, wide):
    shape = (len(planes) * 2 * 3, side, wide)
    return [(shape, bf16)] * 2 + [(shape, f32)] * 2


def ffn_backward(
    layer, seg, rows, lengths, spot, d_pooled, hidden, own, other, active, slope, groups, order,
    params, sets,
):
    side, wide = groups[0].shape[1:]
    count = hidden.shape[0]
    if sets is None:
        results = [((FFN_GROUPS, side, wide), bf16)]
    else:
        results = [item for planes in sets for item in plane_shapes(planes, side, wide)]
    return call(
        partial(ffn_backward_body, seg, order, sets, len(groups)),
        count // rows,
        [
            SMEM,
            SMEM,
            whole(d_pooled.shape),
            by_rows(rows, MODEL_WIDTH),
            by_rows(rows, MODEL_WIDTH),
            by_rows(rows, MODEL_WIDTH),
            by_rows(rows, UNITS),
            by_rows(rows, UNITS),
            whole(params.shape),
        ]
        + [ANY] * len(groups),
        [
            by_rows(rows, MODEL_WIDTH),
            by_rows(rows, MODEL_WIDTH),
            fixed((8, MODEL_WIDTH)),
            fixed((1, UNITS)),
        ]
        + [ANY] * len(results),
        [
            ((count, MODEL_WIDTH), f32),
            ((count, MODEL_WIDTH), bf16),
            ((8, MODEL_WIDTH), f32),
            ((1, UNITS), f32),
        ]
        + results,
        [
            pltpu.VMEM((MODEL_WIDTH, UNITS), bf16),
            pltpu.VMEM((UNITS, MODEL_WIDTH), bf16),
            pltpu.VMEM((MODEL_WIDTH, UNITS), f32),
            pltpu.VMEM((UNITS, MODEL_WIDTH), f32),
            pltpu.SemaphoreType.DMA((FFN_GROUPS,)),
        ],
        us=4.8 * count / 256,
        name=f"ffn_backward_{layer}",
    )(lengths, spot, d_pooled, hidden, own, other, active, slope, params, *groups)


def attention_backward(
    layer, seg, rows, first, blocks, lengths, spot, carried, back_own, back_other, state, own,
    other, qkv, context, logs, groups, order, params, planes=None, buffers=(), carry=(),
    carry_out=False,
):
    side, wide = groups[0].shape[1:]
    count = blocks * rows
    wides = by_rows(rows, MODEL_WIDTH, first)
    out = by_rows(rows, MODEL_WIDTH)
    mats = [((MODEL_WIDTH, 3 * HALF), f32), ((HALF, MODEL_WIDTH), f32)]
    sums = [((8, MODEL_WIDTH), f32), ((1, 3 * HALF), f32)]
    aliases = {}
    if carry_out:
        results = mats
    elif planes is None:
        results = [((ATTENTION_GROUPS, side, wide), bf16)]
    else:
        results = plane_shapes(planes, side, wide)
        before = 12 + len(groups) + len(carry)
        aliases = {before + at: 4 + at for at in range(len(results))}
    return call(
        partial(
            attention_backward_body, seg, order, planes, bool(carry), carry_out, len(groups)
        ),
        blocks,
        [
            SMEM,
            SMEM,
            wides,
            wides,
            wides,
            wides,
            wides,
            wides,
            by_rows(rows, 3 * HALF, first),
            by_rows(rows, HALF, first),
            by_rows(rows, 2 * HD, first),
            whole(params.shape),
        ]
        + [ANY] * len(groups)
        + ([ANY, ANY] + [whole(shape) for shape, _ in sums] if carry else [])
        + [ANY] * len(buffers),
        [out, out] + [fixed(shape) for shape, _ in sums] + [ANY] * len(results),
        [((count, MODEL_WIDTH), f32), ((count, MODEL_WIDTH), bf16)] + sums + results,
        [
            pltpu.VMEM((MODEL_WIDTH, 3 * HALF), bf16),
            pltpu.VMEM((HALF, MODEL_WIDTH), bf16),
            pltpu.VMEM((MODEL_WIDTH, 3 * HALF), f32),
            pltpu.VMEM((HALF, MODEL_WIDTH), f32),
            pltpu.SemaphoreType.DMA((ATTENTION_GROUPS,)),
        ],
        us=5.8 * blocks,
        name=f"attention_backward_{layer}_{first}",
        alias=aliases,
    )(
        lengths, spot, carried, back_own, back_other, state, own, other, qkv, context, logs,
        params, *groups, *carry, *buffers,
    )


def tall_rows(value):
    return 512 if value.shape[0] % 512 == 0 else 256


def expand(rows, slots, fetched):
    count = slots.shape[0]
    return call(
        expand_body,
        count // rows,
        [by_rows(rows, 1), whole(fetched.shape)],
        [by_rows(rows, HALF)],
        [((count, HALF), bf16)],
        us=10.0,
        name="expand",
    )(slots, fetched)[0]


def embed_backward(
    segs, rows, q_parts, p_parts, smalls, mine, theirs, slots, spot, params, parts, width
):
    place = mine.shape[0] // rows - 1
    at_place = pl.BlockSpec((rows, HALF), lambda i: (place, 0), pipeline_mode=pl.Buffered(1))
    blocks = slots.shape[0]
    sources = [q_parts] + list(zip(*p_parts))
    starts, specs, start = [], [], 0
    for source in sources:
        count = source[0].shape[0] // rows
        spec = pl.BlockSpec(
            (rows, MODEL_WIDTH),
            lambda i, start=start, count=count: (jnp.clip(i - start, 0, count - 1), 0),
        )
        specs += [spec] * 3
        starts.append(start)
        start += count
    return call(
        partial(embed_backward_body, segs[:1] + segs[1:] * len(p_parts[0]), tuple(starts), parts),
        blocks,
        specs
        + [whole(value.shape) for value in smalls]
        + [
            by_rows(rows, HALF),
            by_rows(rows, HALF),
            at_place,
            at_place,
            pl.BlockSpec((1, 1, rows), lambda i: (i, 0, 0)),
            SMEM,
            whole(params.shape),
        ],
        [fixed((parts * width, HALF)), fixed((8, MODEL_WIDTH))],
        [((parts * width, HALF), bf16), ((8, MODEL_WIDTH), f32)],
        [pltpu.VMEM((rows, HALF), f32), pltpu.VMEM((parts * width, HALF), f32)],
        us=20.0,
        name="embed_backward",
    )(
        *[part for source in sources for part in source], *smalls, mine, theirs, mine, theirs,
        slots, spot, params,
    )


def pair_blocks(blocks):
    count, side = blocks.shape[0], blocks.shape[-1]
    return (
        blocks.reshape(count // GROUP, GROUP, side, side)
        .transpose(0, 2, 1, 3)
        .reshape(count // GROUP, side, GROUP * side)
    )


def split_pairs(groups):
    count, side = groups.shape[0], groups.shape[1]
    return (
        groups.reshape(count, side, GROUP, side)
        .transpose(0, 2, 1, 3)
        .reshape(count * GROUP, side, side)
    )


def other_core(value):
    return lax.ppermute(value, "tp", [(0, 1), (1, 0)])


def to_all(value, count):
    return lax.all_to_all(jnp.broadcast_to(value[None], (count,) + value.shape), "blk", 0, 0)


def slot_map(present):
    low = jnp.triu(jnp.ones((LANES, LANES), jnp.bfloat16))
    inner = jnp.einsum(
        "ohl,lm->ohm", present.astype(jnp.bfloat16), low, preferred_element_type=jnp.float32
    )
    totals = inner[..., -1]
    before = jnp.cumsum(totals, axis=1) - totals
    ranks = jnp.where(present, inner + before[..., None] - 1.0, -1.0)
    return ranks, jnp.sum(totals, axis=1)


def pick(slots, start, width):
    places = jnp.arange(width, dtype=jnp.float32)
    places = jnp.where(places < SLOTS, places + start, -2.0)
    flat = slots.reshape(slots.shape[0], 1, -1)
    return (flat == places[None, :, None]).astype(jnp.bfloat16)


def pack_body(blocks, out):
    out[0] = jnp.concatenate([blocks[at] for at in range(GROUP)], axis=1).astype(bf16)


def pack(blocks):
    amount, side = blocks.shape[1], blocks.shape[-1]
    return call(
        pack_body,
        amount // GROUP,
        [pl.BlockSpec((None, GROUP, side, side), lambda i: (0, i, 0, 0))],
        [pl.BlockSpec((1, side, GROUP * side), lambda i: (i, 0, 0))],
        [((amount // GROUP, side, GROUP * side), bf16)],
        us=3.0,
        name="pack",
    )(blocks)[0]


def loss_body(asked, codes, positive, d_asked, d_codes, numbers):
    def full(a, b, contract=((1,), (0,))):
        return lax.dot_general(
            a, b, (contract, ((), ())), precision=PRECISION_MAX, preferred_element_type=f32
        )

    scale = 2.0 * MODEL_WIDTH ** (-0.5)
    asks, words = asked[...], codes[...]
    hashed = jnp.tanh(asks)
    dense = full(asks, words, NT) * scale
    binary = full(hashed, words, NT) * scale
    wanted = positive[...]
    columns = lax.broadcasted_iota(jnp.int32, dense.shape, 1)
    hit = columns == wanted
    valid = (wanted >= 0).astype(f32)
    top = jnp.max(dense, axis=1, keepdims=True)
    expo = jnp.exp(dense - top)
    size = jnp.sum(expo, axis=1, keepdims=True)
    cross = top + jnp.log(size) - jnp.sum(jnp.where(hit, dense, 0.0), axis=1, keepdims=True)
    anchor = jnp.sum(jnp.where(hit, binary, 0.0), axis=1, keepdims=True)
    margin = 1.0 - anchor + binary
    small = jnp.exp(-jnp.abs(margin))
    soft = jnp.maximum(margin, 0.0) + jnp.log1p(small)
    others = 1.0 / (dense.shape[1] - 1)
    ranking = jnp.sum(jnp.where(hit, 0.0, soft), axis=1, keepdims=True) * others
    numbers[0:1, :] = jnp.broadcast_to(total(valid * (cross + ranking)), (1, LANES))
    numbers[1:2, :] = jnp.broadcast_to(total(valid), (1, LANES))
    d_dense = valid * (expo / size - hit.astype(f32)) * scale
    rise = jnp.where(margin >= 0, 1.0, small) / (1.0 + small)
    pull = jnp.where(hit, 0.0, rise) * (valid * others)
    d_binary = (pull - jnp.where(hit, jnp.sum(pull, axis=1, keepdims=True), 0.0)) * scale
    d_asked[...] = full(d_dense, words) + full(d_binary, words) * (1.0 - hashed * hashed)
    d_codes[...] = full(d_dense, asks, TN) + full(d_binary, hashed, TN)


def loss_and_back(asked, codes, positive):
    d_asked, d_codes, numbers = call(
        loss_body,
        1,
        [fixed(asked.shape), fixed(codes.shape), fixed(positive.shape)],
        [fixed(asked.shape), fixed(codes.shape), fixed((8, LANES))],
        [(asked.shape, f32), (codes.shape, f32), ((8, LANES), f32)],
        us=5.0,
        name="loss",
    )(asked, codes, positive)
    return numbers[0, 0], numbers[1, 0], d_asked, d_codes


def halves_of(value):
    high = value.astype(bf16)
    return high, (value - high.astype(f32)).astype(bf16)


def near_full(a, b, contract=((1,), (0,))):
    return dot(a[0], b[0], contract) + (dot(a[0], b[1], contract) + dot(a[1], b[0], contract))


def block_products_body(
    paired, inverse, left, right, *rest
):
    parts, (scaled, square, turned, rows, squares) = rest[:-5], rest[-5:]

    @pl.when(pl.program_id(0) == 0)
    def _():
        squares[...] = jnp.zeros_like(squares)

    side = left.shape[-1]
    for at in range(left.shape[0]):
        grad = sum(
            (part[0][:, at * side : (at + 1) * side] if paired else part[at]).astype(f32)
            for part in parts
        )
        grad = grad * inverse[0]
        scaled[at] = grad
        grad_parts = halves_of(grad)
        square[at] = near_full(grad_parts, grad_parts, NT)
        rows[at] = near_full(grad_parts, grad_parts, TN)
        inner = near_full(grad_parts, halves_of(right[at]))
        turned[at] = near_full(halves_of(left[at]), halves_of(inner))
        squares[...] += jnp.broadcast_to(jnp.sum(grad * grad, axis=0, keepdims=True), (8, side))


def block_products(paired, parts, inverse, left, right):
    amount, side = left.shape[1], left.shape[-1]
    per = GROUP if paired else 1
    four = pl.BlockSpec((None, per, side, side), lambda i: (0, i, 0, 0))
    three = pl.BlockSpec((per, side, side), lambda i: (i, 0, 0))
    given = pl.BlockSpec((1,) + parts[0].shape[1:], lambda i: (i, 0, 0))
    return call(
        partial(block_products_body, paired),
        amount // per,
        [SMEM, four, four] + [given] * len(parts),
        [three] * 4 + [fixed((8, side))],
        [((amount, side, side), f32)] * 4 + [((8, side), f32)],
        us=10.0,
        name="block_products",
    )(inverse, left, right, *parts)


def block_update_body(
    factor, scaled, square, rows, turned, left, right, blocks, grads, left_new, right_new, new
):
    scale = factor[0]
    grads[...] = scaled[...] * scale
    left_new[...] = STAT_DECAY * left[...] + ((1.0 - STAT_DECAY) * scale * scale) * square[...]
    right_new[...] = STAT_DECAY * right[...] + ((1.0 - STAT_DECAY) * scale * scale) * rows[...]
    value = blocks[...]
    new[...] = value - SHAMPOO_RATE * (turned[...] * scale + WEIGHT_DECAY * value)


def block_update(factor, scaled, square, rows, turned, left, right, blocks):
    amount, side = left.shape[1], left.shape[-1]
    per = 3 if amount % 3 == 0 else 1
    four = pl.BlockSpec((None, per, side, side), lambda i: (0, i, 0, 0))
    three = pl.BlockSpec((per, side, side), lambda i: (i, 0, 0))
    return call(
        block_update_body,
        amount // per,
        [SMEM] + [three] * 4 + [four] * 3,
        [four] * 4,
        [(left.shape, f32)] * 4,
        us=9.0,
        name="block_update",
    )(factor, scaled, square, rows, turned, left, right, blocks)


class Slice:
    def __init__(self):
        me = lax.axis_index("blk")
        self.x, self.y, self.z = me % 2, me // 2 % 2, me // 4

    @staticmethod
    def over_x(value):
        return lax.ppermute(value, "blk", [(at, at ^ 1) for at in range(16)])

    @staticmethod
    def over_y(value):
        return lax.ppermute(value, "blk", [(at, at ^ 2) for at in range(16)])

    @staticmethod
    def over_z(value, pairs):
        return lax.ppermute(
            value, "blk", [(4 * a + at, 4 * b + at) for a, b in pairs for at in range(4)]
        )


def choose_at(value, index, axis):
    return lax.dynamic_index_in_dim(value, index, axis, keepdims=False)


def add(*values):
    return sum(value.astype(f32) for value in values)


def after(value, *others):
    return lax.optimization_barrier((value,) + others)[0]


def plane_first(links, send_one, send_two, keep_one, keep_two):
    return keep_one, links.over_y(send_one), keep_two, links.over_x(send_two)


def plane_second(links, one, got_one, two, got_two):
    def both(kept, got, index):
        shape = (-1, 2, 3) + kept.shape[1:]
        return add(*(choose_at(part.reshape(shape), index, 1) for part in (kept, got)))

    last_one = links.over_x(both(one, got_one, 1 - links.x).astype(bf16))
    last_two = links.over_y(both(two, got_two, 1 - links.y).astype(bf16))
    return both(one, got_one, links.x), last_one, both(two, got_two, links.y), last_two


def plane_total(one, last_one, two, last_two):
    return jnp.concatenate([add(one, last_one), add(two, last_two)], axis=1)


def column_start(links, plane, pairs):
    return links.over_z(plane.astype(bf16), pairs)


def column_step(links, at_end, first, others, pairs):
    return links.over_z(jnp.where(at_end, first, others).astype(bf16), pairs)


def own_column(links, planes):
    z = links.z
    return jnp.where(
        z < 2, jnp.where(z == 0, planes[0], planes[1]), jnp.where(z == 2, planes[2], planes[3])
    )


def adamw(weight, moment, second, grad):
    moment = BETA_ONE * moment + (1.0 - BETA_ONE) * grad
    second = BETA_TWO * second + (1.0 - BETA_TWO) * grad * grad
    update = (
        moment / (1.0 - BETA_ONE**STEP) / (jnp.sqrt(second / (1.0 - BETA_TWO**STEP)) + ADAM_EPS)
    )
    return (moment, second, weight - ADAM_RATE * (update + WEIGHT_DECAY * weight))


def on_device(
    q_tokens,
    p_tokens,
    q_lengths,
    p_lengths,
    positive,
    table,
    table_moment,
    table_second,
    blocks,
    left_stats,
    right_stats,
    left_roots,
    right_roots,
    vectors,
    vector_moment,
    vector_second,
    shared,
    shared_moment,
    shared_second,
):
    parts = lax.axis_size("blk")
    me, core = lax.axis_index("blk"), lax.axis_index("tp")
    rows_here, half = table.shape
    side = blocks.shape[-1]
    per_device = blocks.shape[1]
    even = per_device % GROUP == 0
    own_blocks = blocks[0].astype(bf16)
    in_order = list(range(ATTENTION_GROUPS + FFN_GROUPS))
    known = parts == 16 and even
    if known:
        links = Slice()
        own_groups = pack(blocks)
        at_z, over = links.z, links.over_z
        spot = jnp.stack(
            [links.x, links.y, (at_z == 0).astype(jnp.int32), (at_z == 3).astype(jnp.int32), core]
        )
        down_one, down_own = over(own_groups, [(3, 2), (2, 1)]), over(own_groups, [(2, 3)])
        up_one, up_own = over(own_groups, [(0, 1), (1, 2)]), over(own_groups, [(1, 0)])
    elif even:
        groups = lax.all_gather(pair_blocks(own_blocks), "blk", axis=0, tiled=True)
    else:
        groups = pair_blocks(lax.all_gather(own_blocks, "blk", axis=0, tiled=True))
    if not known:
        spot = jnp.zeros((5,), jnp.int32).at[4].set(core)
        layer_groups = [(groups[: len(in_order)],), (groups[len(in_order) :],)]
        orders = [in_order, in_order]

    q_live = (jnp.arange(q_tokens.shape[1])[None, :] < q_lengths[:, None]).reshape(-1)
    p_live = (jnp.arange(p_tokens.shape[1])[None, :] < p_lengths[:, None]).reshape(-1)
    tokens = jnp.concatenate([q_tokens.reshape(-1), p_tokens.reshape(-1)])
    live = jnp.concatenate([q_live, p_live])
    tall = -(-rows_here // LANES)
    owner = tokens // rows_here
    inside = tokens - owner * rows_here
    high = jnp.where(live, owner * tall + inside // LANES, -1)
    high_hot = (high[:, None] == jnp.arange(parts * tall)[None, :]).astype(bf16)
    low_hot = (inside[:, None] % LANES == jnp.arange(LANES)[None, :]).astype(bf16)
    uses = jnp.einsum("th,tl->hl", high_hot, low_hot, preferred_element_type=f32)
    present = (uses > 0).reshape(parts, tall, LANES)
    slots, wanted = slot_map(present)
    token_slot = jnp.sum(
        jnp.dot(high_hot.astype(f32), slots.reshape(-1, LANES), precision=PRECISION_MAX) * low_hot,
        axis=1,
    )
    rounds_here = jnp.ceil(jnp.max(wanted) / SLOTS)

    small = jnp.concatenate(
        [
            vectors.astype(bf16).reshape(-1),
            shared.astype(bf16).reshape(-1),
            rounds_here.astype(bf16)[None],
        ]
    )
    small_size = -(-small.shape[0] // LANES) * LANES
    small = jnp.pad(small, (0, small_size - small.shape[0])).reshape(-1, LANES)
    table_low = jnp.pad(table.astype(bf16), ((0, tall * LANES - rows_here), (0, 0)))
    length = p_tokens.shape[1]
    q_length = q_tokens.shape[1]
    share = length // parts
    margin = jnp.zeros((length, half), bf16)
    first_place = jnp.clip(VOCAB - me * rows_here + length, 0, rows_here + length)
    places_here = lax.dynamic_slice_in_dim(
        jnp.concatenate([margin, table_low[:rows_here], margin]), first_place, length, 0
    )
    asks = jnp.concatenate(
        [
            present.astype(bf16),
            jnp.broadcast_to(small[None], (parts,) + small.shape),
            places_here.reshape(parts, share * half // LANES, LANES),
        ],
        axis=1,
    )
    if known:
        asks, down_one, down_own, up_one, up_own = lax.optimization_barrier(
            (asks, down_one, down_own, up_one, up_own)
        )
        down_two, up_two = over(down_one, [(1, 0), (2, 1)]), over(up_one, [(2, 3), (1, 2)])
    asks = lax.all_to_all(asks, "blk", 0, 0)
    if known:
        asks, down_two, up_two = lax.optimization_barrier((asks, down_two, up_two))
        down_three, up_three = over(down_two, [(1, 0)]), over(up_two, [(2, 3)])
        pick_at = lambda *values: jnp.where(
            at_z < 2,
            jnp.where(at_z == 0, values[0], values[1]),
            jnp.where(at_z == 2, values[2], values[3]),
        )
        later_one = pick_at(down_two, down_one, own_groups, own_groups)
        near_one = gather_near(links, later_one)
    asked_slots, _ = slot_map(asks[:, :tall] > 0)
    place_share = jnp.sum(asks[:, tall + small.shape[0] :].astype(f32), axis=0).astype(bf16)
    place_share = place_share.reshape(share, half)
    small = asks[:, tall : tall + small.shape[0]].reshape(parts, -1)
    vector_part, shared_part = vectors.shape[2], shared.shape[1]
    vector_size, shared_size = vectors.size, shared.size
    bias_all = (
        small[:, :vector_size]
        .reshape(parts, LAYERS, vector_part)
        .transpose(1, 0, 2)
        .reshape(LAYERS, -1)
        .astype(f32)
    )
    params_all = (
        small[:, vector_size : vector_size + shared_size]
        .reshape(parts, -1, shared_part)
        .transpose(1, 0, 2)
        .reshape(-1, parts * shared_part)
        .astype(f32)
    )
    rounds = jnp.max(small[:, vector_size + shared_size].astype(f32)).astype(jnp.int32)

    per_part = -(-(LAYERS * (vectors.shape[2] * parts // half) + 2 * shared.shape[0]) // parts)
    width = -(-(SLOTS + share + per_part) // 16) * 16

    def choose(start):
        return pick(asked_slots, start, width)

    def serve(chosen):
        return jnp.einsum("sjr,rc->sjc", chosen, table_low, preferred_element_type=f32).astype(bf16)

    def places_of(start):
        place = token_slot - start
        fits = (high >= 0) & (place >= 0) & (place < SLOTS)
        return jnp.where(fits, owner * width + place.astype(jnp.int32), -1)

    def spread(start):
        return (places_of(start)[:, None] == jnp.arange(parts * width)[None, :]).astype(bf16)

    places_first = places_of(0.0)
    place_at = jnp.arange(length)
    places_first = jnp.concatenate(
        [places_first, place_at // share * width + SLOTS + place_at % share]
    )
    place_rows = places_first[: tokens.shape[0]].reshape(-1, 1, length)
    place_columns = places_first[:, None]

    sent = jnp.concatenate(
        [
            serve(choose(0.0))[:, :SLOTS],
            jnp.broadcast_to(place_share[None], (parts, share, half)),
            jnp.zeros((parts, width - SLOTS - share, half), bf16),
        ],
        axis=1,
    )
    if known:
        sent, down_three, up_three, *near_one = lax.optimization_barrier(
            (sent, down_three, up_three) + near_one
        )
        far_one = gather_far(links, *near_one)
        later_two = pick_at(down_three, down_two, down_one, down_own)
        near_two = gather_near(links, later_two)
    fetched = lax.all_to_all(sent, "blk", 0, 0)
    if known:
        place_columns, place_rows, far_two, near_two = lax.optimization_barrier(
            (place_columns, place_rows, far_one, near_two)
        )
        far_one = far_two
        far_two = gather_far(links, *near_two)
    halves = expand(length, place_columns, fetched.reshape(-1, half))

    def fetch_more(carry):
        done, total = carry
        start = (done * SLOTS).astype(f32)
        more = lax.all_to_all(serve(choose(start)), "blk", 0, 0).reshape(-1, half)
        more = jnp.dot(spread(start), more, preferred_element_type=f32).astype(bf16)
        return done + 1, total.at[: tokens.shape[0]].add(more)

    if known:
        halves, *far_two = lax.optimization_barrier((halves,) + far_two)
        layer_groups = [
            None, (later_one, *near_one, *far_one, later_two, *near_two, *far_two)
        ]
        orders = [0, 1]
        early_one = pick_at(own_groups, own_groups, up_one, up_two)
        early_two = pick_at(up_own, up_one, up_two, up_three)
    halves = lax.while_loop(lambda c: c[0] < rounds, fetch_more, (jnp.int32(1), halves))[1]
    others = other_core(halves)
    embed_params = params_all[:2]
    q_blocks, p_blocks = q_tokens.size // length, p_tokens.size // length

    def first_half(layer, seg, first, count, lengths):
        bias = bias_all[layer : layer + 1]
        params = params_all[2 + 6 * layer : 8 + 6 * layer]
        return [layer, seg, lengths, bias, params] + list(attention_forward(
            layer, seg, length, count, first, lengths, spot, halves, others,
            layer_groups[layer], orders[layer], bias, embed_params,
        ))

    def second_half(kept):
        layer, seg, lengths, bias, params, state, qkv, context, logs, own_one = kept
        other_one = other_core(own_one)
        return kept + [other_one] + list(ffn_forward(
            layer, tall_rows(state), spot, state, own_one, other_one, layer_groups[layer],
            orders[layer], bias, params,
        ))

    def pool_of(kept):
        layer, seg, lengths, _, params = kept[:5]
        hidden, _, _, own_two = kept[11:]
        other_two = other_core(own_two)
        kept.append(other_two)
        return pool_forward(layer, seg, length, lengths, hidden, own_two, other_two, params)

    if known:
        near_one = gather_near(links, early_one)
    p_kept = first_half(1, length, q_blocks, p_blocks, p_lengths)
    if known:
        p_kept[-1], *near_one = lax.optimization_barrier((p_kept[-1],) + near_one)
        far_one = gather_far(links, *near_one)
        near_two = gather_near(links, early_two)
    p_kept = second_half(p_kept)
    if known:
        p_kept[-1], *four = lax.optimization_barrier((p_kept[-1],) + far_one + near_two)
        far_one, near_two = four[:2], four[2:]
        far_two = gather_far(links, *near_two)
    p_pooled = pool_of(p_kept)
    if known:
        p_pooled, *far_two = lax.optimization_barrier((p_pooled,) + far_two)
        layer_groups[0] = (early_one, *near_one, *far_one, early_two, *near_two, *far_two)
    q_kept = second_half(first_half(0, q_length, 0, q_blocks, q_lengths))
    codes_local = jnp.tanh(p_pooled)
    codes_low = codes_local.astype(bf16)
    codes = to_all(codes_low, parts)
    q_kept[-1], codes = lax.optimization_barrier((q_kept[-1], codes))
    pooled = [pool_of(q_kept), p_pooled]
    asked_local = pooled[0]
    codes = codes.reshape(-1, MODEL_WIDTH).astype(f32)
    every = to_all(
        jnp.concatenate(
            [
                asked_local,
                jnp.pad(positive.astype(f32)[None], ((0, 0), (0, MODEL_WIDTH - positive.shape[0]))),
            ]
        ),
        parts,
    )
    q_part, p_part = asked_local.shape[0], codes_local.shape[0]
    asked = every[:, :q_part].reshape(-1, MODEL_WIDTH)
    positives = every[:, q_part, :q_part].reshape(-1).astype(jnp.int32)
    loss_sum, positives_count, d_asked, d_codes = loss_and_back(asked, codes, positives[:, None])
    d_asked = lax.dynamic_slice_in_dim(d_asked, me * q_part, q_part, 0)
    d_codes = lax.dynamic_slice_in_dim(d_codes, me * p_part, p_part, 0)
    d_passages = d_codes * (1.0 - codes_local * codes_local)
    def ffn_back(kept, d_pooled, sets):
        (layer, seg, lengths, bias, params, state, qkv, context, logs, own_one, other_one, hidden,
         active, slope, own_two, other_two) = kept
        return ffn_backward(
            layer, seg, tall_rows(hidden), lengths, spot, d_pooled, hidden, own_two, other_two, active, slope,
            layer_groups[layer], orders[layer], params, sets,
        )

    def attention_back(kept, base, back_own, back_other, first, count, **more):
        (layer, seg, lengths, bias, params, state, qkv, context, logs, own_one, other_one) = kept[:11]
        return attention_backward(
            layer, seg, length, first, count, lengths[first:] if first else lengths, spot, base,
            back_own, back_other, state, own_one, other_one, qkv, context, logs,
            layer_groups[layer], orders[layer], params, **more,
        )

    q_base, q_back, q_ffn_sums, q_up_bias, *q_ffn = ffn_back(
        q_kept, d_asked, ((0, 1),) if known else None
    )
    q_state, q_state_own, q_sums, q_bias, *q_attention = attention_back(
        q_kept, q_base, q_back, other_core(q_back), 0, q_blocks,
        **(dict(planes=(0, 1), buffers=q_ffn) if known else {}),
    )
    p_base, p_back, p_ffn_sums, p_up_bias, *p_ffn = ffn_back(
        p_kept, after(d_passages, q_sums), ((0,), (1,)) if known else None
    )
    if known:
        early = p_blocks // 2
        q_first = plane_first(links, *q_attention)
        top_first = plane_first(links, *p_ffn[4:])
        p_back, *q_first = lax.optimization_barrier((p_back,) + q_first)
        p_back_other = other_core(p_back)
        q_second = plane_second(links, *q_first)
        state_one, own_one, *carry = attention_back(
            p_kept, p_base, p_back, p_back_other, 0, early, carry_out=True
        )
        carry = carry[2:] + carry[:2]
        other_one = other_core(own_one)
        carry[2], *eight = lax.optimization_barrier((carry[2],) + q_second + top_first)
        q_planes = plane_total(*eight[:4])
        top_second = plane_second(links, *eight[4:])
        down = column_start(links, q_planes[0], [(3, 2)])
        state_two, own_two, p_sums, p_bias, *low = attention_back(
            p_kept, p_base, p_back, p_back_other, early, p_blocks - early, carry=carry,
            planes=(0,), buffers=p_ffn[:4],
        )
        own_two, down, *top_second = lax.optimization_barrier((own_two, down) + top_second)
        top_plane = plane_total(*top_second)[0]
        other_two = other_core(own_two)
        up = column_start(links, top_plane, [(0, 1)])
        down = column_step(
            links, links.z == 3, q_planes[1], add(q_planes[0], down), [(3, 2), (2, 1)]
        )
        low_first = plane_first(links, *low)
        state_p = ((state_one, state_two), (own_one, own_two), (other_one, other_two))
        low_first = plane_first(links, *low)
    else:
        p_back_other = other_core(p_back)
        state_one, own_one, p_sums, p_bias, *p_attention = attention_back(
            p_kept, p_base, p_back, p_back_other, 0, p_blocks
        )
        state_p = ((state_one,), (own_one,), (other_core(own_one),))
    smalls = (
        q_bias, q_up_bias, p_bias, p_up_bias, q_sums, q_ffn_sums, p_sums, p_ffn_sums
    )
    vector_rows = LAYERS * vector_part * parts // half
    state_parts = [
        (q_state, q_state_own, other_core(q_state_own)),
        state_p,
    ]
    picked, _ = embed_backward(
        (q_length, length), length, state_parts[0], state_parts[1], smalls, halves, others, place_rows,
        spot, embed_params, parts, width,
    )
    if known:
        picked, up, down, *low_first = lax.optimization_barrier((picked, up, down) + low_first)

    def gather_up(start):
        return embed_backward(
            (q_length, length), length, state_parts[0], state_parts[1], smalls, halves, others,
            places_of(start).reshape(-1, 1, length), spot, embed_params, parts, width,
        )[0].reshape(parts, width, half)

    def put_back(chosen, received):
        return jnp.einsum("sjr,sjc->rc", chosen, received, preferred_element_type=f32)[:rows_here]

    sent = picked.reshape(parts, width, half)
    got = lax.all_to_all(sent, "blk", 0, 0)
    token_grad = put_back(choose(0.0), got)

    def send_more(carry):
        done, total = carry
        start = (done * SLOTS).astype(f32)
        more = lax.all_to_all(gather_up(start), "blk", 0, 0)
        return done + 1, total + put_back(choose(start), more)

    token_grad = lax.while_loop(lambda c: c[0] < rounds, send_more, (jnp.int32(1), token_grad))[1]
    rest = jnp.sum(got[:, SLOTS : SLOTS + share + per_part].astype(f32), axis=0)
    if known:
        low_plane = plane_total(*plane_second(links, *low_first))[0]
        z = links.z
        planes = [q_planes[0], q_planes[1], low_plane, top_plane]
        up = column_step(links, z == 0, low_plane, add(top_plane, up), [(0, 1), (1, 2)])
        down = column_step(
            links, z == 3, low_plane, add(jnp.where(z == 2, q_planes[1], q_planes[0]), down),
            [(3, 2), (2, 1), (1, 0)],
        )
        base = lax.optimization_barrier(
            jnp.where(z == 0, q_planes[1], jnp.where(z == 1, low_plane, top_plane))
        )
        up = links.over_z(
            (base + jnp.where(z == 0, 0.0, up.astype(f32))).astype(bf16),
            [(0, 1), (1, 2), (2, 3)],
        )
        grad_parts = (own_column(links, planes), up, down)
    else:
        all_groups = jnp.concatenate(q_attention + q_ffn + p_attention + p_ffn, axis=0)
        if not even:
            all_groups = split_pairs(all_groups)
        grad_parts = (lax.psum_scatter(all_groups, "blk", scatter_dimension=0, tiled=True),)
    inverse = 1.0 / positives_count
    rest = rest * inverse
    row_index = me * per_part + jnp.arange(per_part)
    counted = ((row_index < vector_rows) | (core == 0)).astype(f32)
    squares = (
        jnp.sum(rest[:share] ** 2)
        + jnp.sum(rest[share:] ** 2 * counted[:, None])
        + jnp.sum((token_grad * inverse) ** 2)
    )
    rest = to_all(rest, parts)
    if known:
        squares, *grad_parts = lax.optimization_barrier((squares,) + grad_parts)
    scaled, square, turned, row_square, block_squares = block_products(
        even, grad_parts, inverse[None], left_roots, right_roots
    )
    block_squares, rest = lax.optimization_barrier((block_squares, rest))
    place_grads = rest[:, :share].reshape(length, half)
    small_grads = rest[:, share:].reshape(-1, half)
    grad_vectors = lax.dynamic_slice_in_dim(
        small_grads[:vector_rows].reshape(LAYERS, -1), me * vector_part, vector_part, 1
    )[None]
    shared_rows = shared.shape[0]
    grad_shared = lax.dynamic_slice_in_dim(
        jnp.concatenate(
            [
                small_grads[vector_rows : vector_rows + shared_rows],
                small_grads[vector_rows + shared_rows : vector_rows + 2 * shared_rows],
            ],
            axis=1,
        ),
        me * shared_part,
        shared_part,
        1,
    )
    margin = jnp.zeros((rows_here, half), f32)
    place_grads = lax.dynamic_slice_in_dim(
        jnp.concatenate([margin, place_grads, margin]),
        jnp.clip(me * rows_here - VOCAB + rows_here, 0, rows_here + length),
        rows_here,
        0,
    )
    table_grad = token_grad * inverse + place_grads
    squares = squares + jnp.sum(block_squares[0])
    devices = parts * 2
    squares = lax.all_to_all(
        jnp.broadcast_to(squares, (devices, 8, LANES)), ("blk", "tp"), 0, 0
    )
    squares = jnp.sum(squares[:, 0, 0])
    grad_norm = jnp.sqrt(squares)
    factor = jnp.minimum(1.0, CLIP / grad_norm)
    block_grads, left_new, right_new, blocks_new = block_update(
        factor[None], scaled, square, row_square, turned, left_stats, right_stats, blocks
    )
    table_moment_new, table_second_new, table_new = adamw(
        table, table_moment, table_second, table_grad * factor
    )
    vector_moment_new, vector_second_new, vectors_new = adamw(
        vectors, vector_moment, vector_second, grad_vectors * factor
    )
    shared_moment_new, shared_second_new, shared_new = adamw(
        shared, shared_moment, shared_second, grad_shared * factor
    )
    return (
        loss_sum,
        positives_count,
        grad_norm,
        block_grads,
        left_new,
        right_new,
        blocks_new,
        table_moment_new,
        table_second_new,
        table_new,
        vector_moment_new,
        vector_second_new,
        vectors_new,
        shared_moment_new,
        shared_second_new,
        shared_new,
    )


def solution(mesh):
    return jax.shard_map(
        on_device,
        mesh=mesh,
        in_specs=(
            P("blk", None),
            P("blk", None),
            P("blk"),
            P("blk"),
            P("blk"),
            P("blk", "tp"),
            P("blk", "tp"),
            P("blk", "tp"),
            P("tp", "blk", None, None),
            P("tp", "blk", None, None),
            P("tp", "blk", None, None),
            P("tp", "blk", None, None),
            P("tp", "blk", None, None),
            P("tp", None, "blk"),
            P("tp", None, "blk"),
            P("tp", None, "blk"),
            P(None, "blk"),
            P(None, "blk"),
            P(None, "blk"),
        ),
        out_specs=(
            P(),
            P(),
            P(),
            P("tp", "blk", None, None),
            P("tp", "blk", None, None),
            P("tp", "blk", None, None),
            P("tp", "blk", None, None),
            P("blk", "tp"),
            P("blk", "tp"),
            P("blk", "tp"),
            P("tp", None, "blk"),
            P("tp", None, "blk"),
            P("tp", None, "blk"),
            P(None, "blk"),
            P(None, "blk"),
            P(None, "blk"),
        ),
        check_vma=False,
    )
```

profile of v0, /device:TPU:0, one launch (start us, length us, event | category | flops | bytes accessed | tf_op | source)
XLA Modules:
  0.0 639.1 jit_solution(5381749296078609441)
XLA Ops:
  23.3 9.3 %collective-permute-done.2 = bf16[6,192,384]{2,1,0:T(8,128)(2,1)} collective-permute-done((bf16[6,192,384]{2,1,0:T(8,128)(2,1)}, bf16[6,192,384]{2,1,0:T(8,128)(2,1)}, u32[]{:S(2)}, u32[]{:S(2)}) %collective-permute-start.2) | collective-permute-done | bytes 884768 | tf_op jit(solution)/shard_map/ppermute | solution.py:1064
  43.1 7.6 %all-to-all-start.2 = ((bf16[16,72,128]{2,1,0:T(8,128)(2,1)}), bf16[16,72,128]{2,1,0:T(8,128)(2,1)S(1)}, u32[]{:S(2)}, u32[]{:S(2)}) async-start(bf16[16,72,128]{2,1,0:T(8,128)(2,1)} %pad_maximum_fusion.1), calls=%async_computation.2 | async-start | bytes 589824 | tf_op jit(solution)/shard_map/all_to_all | solution.py:1221
  50.8 18.0 %all-to-all-done.2 = bf16[16,72,128]{2,1,0:T(8,128)(2,1)S(1)} async-done(((bf16[16,72,128]{2,1,0:T(8,128)(2,1)}), bf16[16,72,128]{2,1,0:T(8,128)(2,1)S(1)}, u32[]{:S(2)}, u32[]{:S(2)}) %all-to-all-start.2) | async-done | bytes 294944 | tf_op jit(solution)/shard_map/all_to_all | solution.py:1221
  92.7 9.8 %all-to-all-start.3 = ((bf16[16,112,384]{2,1,0:T(8,128)(2,1)}), bf16[16,112,384]{2,1,0:T(8,128)(2,1)}, u32[]{:S(2)}, u32[]{:S(2)}) async-start(bf16[16,112,384]{2,1,0:T(8,128)(2,1)} %maximum_maximum_fusion), calls=%async_computation.3 | async-start | bytes 2752512 | tf_op jit(solution)/shard_map/all_to_all | solution.py:1294
  111.8 33.2 %collective-permute-done.10.rest_3_ = bf16[3,192,384]{2,1,0:T(8,128)(2,1)S(1)} collective-permute-done((bf16[3,192,384]{2,1,0:T(8,128)(2,1)S(1)}, bf16[3,192,384]{2,1,0:T(8,128)(2,1)S(1)}, u32[]{:S(2)}, u32[]{:S(2)}) %collective-permute-start.10) | collective-permute-done | bytes 442400 | tf_op jit(solution)/shard_map/ppermute | solution.py:1060
  156.1 9.3 %expand.1 = bf16[2560,384]{1,0:T(8,128)(2,1)S(1)} custom-call(s32[2560,1]{1,0:T(8,128)} %copy.117.slots, bf16[1792,384]{1,0:T(8,128)(2,1)} %bitcast.15.fetched), custom_call_target="tpu_custom_call" | custom-call | flops 1150000000 | bytes 100000 | tf_op jit(solution)/shard_map/expand/pallas_call | solution.py:809
  172.8 20.6 %attention_forward_1.1 = (f32[2048,768]{1,0:T(8,128)}, bf16[2048,1152]{1,0:T(8,128)(2,1)}, bf16[2048,384]{1,0:T(8,128)(2,1)}, f32[2048,128]{1,0:T(8,128)}, bf16[2048,768]{1,0:T(8,128)(2,1)}) custom-call(s32[8]{0:T(128)} %lengths.15, s32[5]{0:T(128)S(1)} %stack.31.spot.refs_22_, bf16[2560,384]{1,0:T(8,128)(2,1)S(1)} %get-tuple-element.956.mine.place_mine.refs_17_.refs_19_, ...), custom_call_target="tpu_custom_call" | custom-call | flops 2300000000 | bytes 200000 | tf_op jit(solution)/shard_map/attention_forward_1/pallas_call | solution.py:594
  202.0 29.8 %ffn_forward_1.1 = (f32[2048,768]{1,0:T(8,128)}, bf16[2048,1536]{1,0:T(8,128)(2,1)}, bf16[2048,1536]{1,0:T(8,128)(2,1)}, bf16[2048,768]{1,0:T(8,128)(2,1)}) custom-call(s32[5]{0:T(128)S(1)} %stack.31.spot.refs_22_, f32[2048,768]{1,0:T(8,128)} %get-tuple-element.442.state, bf16[2048,768]{1,0:T(8,128)(2,1)} %get-tuple-element.443.own, ...), custom_call_target="tpu_custom_call" | custom-call | flops 3496000000 | bytes 304000 | tf_op jit(solution)/shard_map/ffn_forward_1/pallas_call | solution.py:634
  239.1 9.2 %pool_1.1 = f32[8,768]{1,0:T(8,128)} custom-call(s32[8]{0:T(128)} %lengths.15, f32[2048,768]{1,0:T(8,128)} %get-tuple-element.451.hidden, bf16[2048,768]{1,0:T(8,128)(2,1)} %get-tuple-element.452.own, bf16[2048,768]{1,0:T(8,128)(2,1)} %collective-permute-done.24.other, f32[6,768]{1,0:T(8,128)} %slice.188.params), custom_call_target="tpu_custom_call" | custom-call | flops 1012000000 | bytes 88000 | tf_op jit(solution)/shard_map/pool_1/pallas_call | solution.py:670
  262.5 8.1 %ffn_forward_0.1 = (f32[256,768]{1,0:T(8,128)}, bf16[256,1536]{1,0:T(8,128)(2,1)}, bf16[256,1536]{1,0:T(8,128)(2,1)}, bf16[256,768]{1,0:T(8,128)(2,1)}) custom-call(s32[5]{0:T(128)S(1)} %stack.31.spot.refs_22_, f32[256,768]{1,0:T(8,128)} %get-tuple-element.455.state, bf16[256,768]{1,0:T(8,128)(2,1)} %get-tuple-element.456.own, bf16[256,768]{1,0:T(8,128)(2,1)} %copy-done.40, ...), custom_call_target="tpu_custom_call" | custom-call | flops 437000000 | bytes 38000 | tf_op jit(solution)/shard_map/ffn_forward_0/pallas_call | solution.py:634
  285.2 12.1 %all-to-all-done.5 = f32[16,5,768]{2,1,0:T(8,128)S(1)} async-done(((f32[16,5,768]{2,1,0:T(8,128)}), f32[16,5,768]{2,1,0:T(8,128)S(1)}, u32[]{:S(2)}, u32[]{:S(2)}) %all-to-all-start.5) | async-done | bytes 245792 | tf_op jit(solution)/shard_map/all_to_all | solution.py:885
  304.5 12.1 %ffn_backward_0.1 = (f32[256,768]{1,0:T(8,128)}, bf16[256,768]{1,0:T(8,128)(2,1)}, f32[8,768]{1,0:T(8,128)}, f32[1,1536]{1,0:T(1,128)}, bf16[12,192,384]{2,1,0:T...) custom-call(s32[4]{0:T(128)} %lengths.13, ...), custom_call_target="tpu_custom_call" | custom-call | flops 552000000 | bytes 48000 | tf_op jit(solution)/shard_map/ffn_backward_0/pallas_call | solution.py:702
  319.4 11.3 %attention_backward_0_0.1 = (f32[256,768]{1,0:T(8,128)}, bf16[256,768]{1,0:T(8,128)(2,1)}, f32[8,768]{1,0:T(8,128)}, f32[1,1152]{1,0:T(1,128)}, bf16[12,192,384]...) custom-call(s32[4]{0:T(128)} %lengths.13, ...), custom_call_target="tpu_custom_call", output_to_operand_aliasing={{4}: (22, {}), {5}: (23, {}), {6}: (24, {}), {7}: (25, {})} | custom-call | flops 667000000 | bytes 58000 | tf_op jit(solution)/shard_map/attention_backward_0_0/pallas_call | solution.py:763
  333.6 39.0 %ffn_backward_1.1 = (f32[2048,768]{1,0:T(8,128)}, bf16[2048,768]{1,0:T(8,128)(2,1)}, f32[8,768]{1,0:T(8,128)}, f32[1,1536]{1,0:T(1,128)}, bf16[6,192,384]{2,1,0:...) custom-call(s32[8]{0:T(128)} %lengths.15, ...), custom_call_target="tpu_custom_call" | custom-call | flops 4416000000 | bytes 384000 | tf_op jit(solution)/shard_map/ffn_backward_1/pallas_call | solution.py:702
  384.7 26.7 %attention_backward_1_0.1 = (f32[1024,768]{1,0:T(8,128)}, bf16[1024,768]{1,0:T(8,128)(2,1)S(1)}, f32[8,768]{1,0:T(8,128)}, f32[1,1152]{1,0:T(1,128)}, f32[768,1152]{1,0:T(8,128)}, /*index=5*/f32[384,768]{1,0:T(8,128)}) custom-call(s32[8]{0:T(128)} %lengths.15, s32[5]{0:T(128)S(1)} %stack.31.spot.refs_22_, f32[2048,768]{1,0:T(8,128)} %get-tuple-element.482.carried, ...), custom_call_target="tpu_custom_call" | custom-call | flops 2668000000 | bytes 232000 | tf_op jit(solution)/shard_map/attention_backward_1_0/pallas_call | solution.py:763
  430.5 29.3 %attention_backward_1_4.1 = (f32[1024,768]{1,0:T(8,128)}, bf16[1024,768]{1,0:T(8,128)(2,1)}, f32[8,768]{1,0:T(8,128)S(1)}, f32[1,1152]{1,0:T(1,128)S(1)}, bf16[6...) custom-call(s32[4]{0:T(128)} %slice.199.lengths, ...), custom_call_target="tpu_custom_call", output_to_operand_aliasing={{4}: (26, {}), {5}: (27, {}), {6}: (28, {}), {7}: (29, {})} | custom-call | flops 2668000000 | bytes 232000 | tf_op jit(solution)/shard_map/attention_backward_1_4/pallas_call | solution.py:763
  474.9 21.9 %embed_backward.2 = (bf16[1792,384]{1,0:T(8,128)(2,1)}, f32[8,768]{1,0:T(8,128)}) custom-call(f32[256,768]{1,0:T(8,128)} %get-tuple-element.939.refs_0_, bf16[256,768]{1,0:T(8,128)(2,1)S(1)} %copy-done.20, bf16[256,768]{1,0:T(8,128)(2,1)} %collective-permute-done.30.refs_2_, f32[1024,768]{1,0:T(8,128)} %get-tuple-element.942.refs_3_, ...), custom_call_target="tpu_custom_call" | custom-call | flops 2300000000 | bytes 200000 | tf_op jit(solution)/shard_map/embed_backward/pallas_call | solution.py:837
  513.8 14.9 %collective-permute-done.48 = bf16[1,3,192,384]{3,2,1,0:T(8,128)(2,1)S(1)} collective-permute-done((bf16[1,3,192,384]{3,2,1,0:T(8,128)(2,1)S(1)}, bf16[1,3,192,384]{3,2,1,0:T(8,128)(2,1)S(1)}, u32[]{:S(2)}, u32[]{:S(2)}) %collective-permute-start.48) | collective-permute-done | bytes 442400 | tf_op jit(solution)/shard_map/ppermute | solution.py:1060
  547.5 9.0 %collective-permute-done.49 = bf16[6,192,384]{2,1,0:T(8,128)(2,1)} collective-permute-done((bf16[6,192,384]{2,1,0:T(8,128)(2,1)}, bf16[6,192,384]{2,1,0:T(8,128)(2,1)}, u32[]{:S(2)}, u32[]{:S(2)}) %collective-permute-start.49) | collective-permute-done | bytes 884768 | tf_op jit(solution)/shard_map/ppermute | solution.py:1064
  587.0 10.4 %block_products.1 = (f32[12,192,192]{2,1,0:T(8,128)}, f32[12,192,192]{2,1,0:T(8,128)}, f32[12,192,192]{2,1,0:T(8,128)}, f32[12,192,192]{2,1,0:T(8,128)}, f32[8,192]{1,0:T(8,128)}) custom-call(f32[1]{0:T(128)} %bitcast.52.inverse, f32[1,12,192,192]{3,2,1,0:T(8,128)} %left.2, f32[1,12,192,192]{3,2,1,0:T(8,128)} %right.2, ...), custom_call_target="tpu_custom_call" | custom-call | flops 1150000000 | bytes 100000 | tf_op jit(solution)/shard_map/block_products/pallas_call | solution.py:1011
  600.0 7.7 %all-to-all-start.8 = ((f32[32,8,128]{2,1,0:T(8,128)}), f32[32,8,128]{2,1,0:T(8,128)S(1)}, u32[]{:S(2)}, u32[]{:S(2)}) async-start(f32[32,8,128]{2,1,0:T(8,128)} %broadcast_in_dim.128), calls=%async_computation.8 | async-start | bytes 262144 | tf_op jit(solution)/shard_map/all_to_all | solution.py:1550
  607.9 8.1 %all-to-all-done.8 = f32[32,8,128]{2,1,0:T(8,128)S(1)} async-done(((f32[32,8,128]{2,1,0:T(8,128)}), f32[32,8,128]{2,1,0:T(8,128)S(1)}, u32[]{:S(2)}, u32[]{:S(2)}) %all-to-all-start.8) | async-done | bytes 131104 | tf_op jit(solution)/shard_map/all_to_all | solution.py:1550
  619.0 9.5 %multiply_subtract_fusion = (f32[1944,384]{1,0:T(8,128)}, f32[1944,384]{1,0:T(8,128)}, f32[1944,384]{1,0:T(8,128)}) fusion(f32[1944,384]{1,0:T(8,128)} %param.30, f32[]{:T(128)} %min.11, s32[]{:T(128)S(6)} %min.12, f32[1944,384]{1,0:T(8,128)S(1)} %broadcast_in_dim.130, f32[256,384]{1,0:T(8,128)S(1)} %bitcast.196, f32[1944,384]{1,0:T(8,128)} %get-tuple-element.541, ...), kind=kLoop, calls=%fused_computation.45 | loop fusion | flops 17915904 | bytes 24281100 | tf_op jit(solution)/shard_map/sub | solution.py:1120
  628.4 9.2 %block_update.1 = (f32[1,12,192,192]{3,2,1,0:T(8,128)}, f32[1,12,192,192]{3,2,1,0:T(8,128)}, f32[1,12,192,192]{3,2,1,0:T(8,128)}, f32[1,12,192,192]{3,2,1,0:T(8,128)}) custom-call(f32[1]{0:T(128)} %bitcast.53.factor, f32[12,192,192]{2,1,0:T(8,128)} %get-tuple-element.554.scaled, f32[12,192,192]{2,1,0:T(8,128)} %get-tuple-element.555.square, ...), custom_call_target="tpu_custom_call" | custom-call | flops 1035000000 | bytes 90000 | tf_op jit(solution)/shard_map/block_update/pallas_call | solution.py:1038
  (406 shorter events, 253.9 us)
Async XLA Ops:
  92.7 63.5 %all-to-all-start.3 = ((bf16[16,112,384]{2,1,0:T(8,128)(2,1)}), bf16[16,112,384]{2,1,0:T(8,128)(2,1)}, u32[]{:S(2)}, u32[]{:S(2)}) async-start(bf16[16,112,384]{2,1,0:T(8,128)(2,1)} %maximum_maximum_fusion), calls=%async_computation.3 | async-start | bytes 2752512 | tf_op jit(solution)/shard_map/all_to_all | solution.py:1294
  106.5 38.9 %collective-permute-start.12 = (bf16[6,192,384]{2,1,0:T(8,128)(2,1)S(1)}, bf16[6,192,384]{2,1,0:T(8,128)(2,1)}, u32[]{:S(2)}, u32[]{:S(2)}) collective-permute-start(bf16[6,192,384]{2,1,0:T(8,128)(2,1)S(1)} %select_select_fusion.4.rest_5_), channel_id=1, source_target_pairs={{0,2},{2,0},{4,6},{6,4},{8,10},{10,8},{12,14},{14,12},{16,18},{18,... | collective-permute-start | bytes 2654216 | tf_op jit(solution)/shard_map/ppermute | solution.py:1056
  108.6 36.8 %collective-permute-start.13 = (bf16[6,192,384]{2,1,0:T(8,128)(2,1)S(1)}, bf16[6,192,384]{2,1,0:T(8,128)(2,1)}, u32[]{:S(2)}, u32[]{:S(2)}) collective-permute-start(bf16[6,192,384]{2,1,0:T(8,128)(2,1)S(1)} %select_select_fusion.4.rest_5_), channel_id=1, source_target_pairs={{0,4},{2,6},{4,0},{6,2},{8,12},{10,14},{12,8},{14,10},{16,20},{18,... | collective-permute-start | bytes 2654216 | tf_op jit(solution)/shard_map/ppermute | solution.py:1060
  110.2 34.8 %collective-permute-start.10 = (bf16[3,192,384]{2,1,0:T(8,128)(2,1)S(1)}, bf16[3,192,384]{2,1,0:T(8,128)(2,1)S(1)}, u32[]{:S(2)}, u32[]{:S(2)}) collective-permute-start(bf16[3,192,384]{2,1,0:T(8,128)(2,1)S(1)} %slice.173), channel_id=1, source_target_pairs={{0,4},{2,6},{4,0},{6,2},{8,12},{10,14},{12,8},{14,10},{16,20},{18,... | collective-permute-start | bytes 1327112 | tf_op jit(solution)/shard_map/ppermute | solution.py:1060
  110.9 34.5 %collective-permute-start.11 = (bf16[3,192,384]{2,1,0:T(8,128)(2,1)S(1)}, bf16[3,192,384]{2,1,0:T(8,128)(2,1)S(1)}, u32[]{:S(2)}, u32[]{:S(2)}) collective-permute-start(bf16[3,192,384]{2,1,0:T(8,128)(2,1)S(1)} %slice.174), channel_id=1, source_target_pairs={{0,2},{2,0},{4,6},{6,4},{8,10},{10,8},{12,14},{14,12},{16,18},{18,... | collective-permute-start | bytes 1327112 | tf_op jit(solution)/shard_map/ppermute | solution.py:1056
  193.5 38.3 %collective-permute-start.22 = (bf16[6,192,384]{2,1,0:T(8,128)(2,1)S(1)}, bf16[6,192,384]{2,1,0:T(8,128)(2,1)}, u32[]{:S(2)}, u32[]{:S(2)}) collective-permute-start(bf16[6,192,384]{2,1,0:T(8,128)(2,1)S(1)} %get-tuple-element.664.rest_5_), channel_id=1, source_target_pairs={{0,2},{2,0},{4,6},{6,4},{8,10},{10,8},{12,14},{14,12},{16,18},{18,... | collective-permute-start | bytes 2654216 | tf_op jit(solution)/shard_map/ppermute | solution.py:1056
  195.3 36.5 %collective-permute-start.23 = (bf16[6,192,384]{2,1,0:T(8,128)(2,1)S(1)}, bf16[6,192,384]{2,1,0:T(8,128)(2,1)}, u32[]{:S(2)}, u32[]{:S(2)}) collective-permute-start(bf16[6,192,384]{2,1,0:T(8,128)(2,1)S(1)} %get-tuple-element.664.rest_5_), channel_id=1, source_target_pairs={{0,4},{2,6},{4,0},{6,2},{8,12},{10,14},{12,8},{14,10},{16,20},{18,... | collective-permute-start | bytes 2654216 | tf_op jit(solution)/shard_map/ppermute | solution.py:1060
  198.1 33.7 %collective-permute-start.20 = (bf16[3,192,384]{2,1,0:T(8,128)(2,1)}, bf16[3,192,384]{2,1,0:T(8,128)(2,1)S(1)}, u32[]{:S(2)}, u32[]{:S(2)}) collective-permute-start(bf16[3,192,384]{2,1,0:T(8,128)(2,1)} %slice.189), channel_id=1, source_target_pairs={{0,4},{2,6},{4,0},{6,2},{8,12},{10,14},{12,8},{14,10},{16,20},{18,... | collective-permute-start | bytes 1327112 | tf_op jit(solution)/shard_map/ppermute | solution.py:1060
  201.0 30.9 %collective-permute-start.21 = (bf16[3,192,384]{2,1,0:T(8,128)(2,1)}, bf16[3,192,384]{2,1,0:T(8,128)(2,1)}, u32[]{:S(2)}, u32[]{:S(2)}) collective-permute-start(bf16[3,192,384]{2,1,0:T(8,128)(2,1)} %slice.190), channel_id=1, source_target_pairs={{0,2},{2,0},{4,6},{6,4},{8,10},{10,8},{12,14},{14,12},{16,18},{18,... | collective-permute-start | bytes 1327112 | tf_op jit(solution)/shard_map/ppermute | solution.py:1056
  330.7 41.9 %collective-permute-start.31 = (bf16[12,192,384]{2,1,0:T(8,128)(2,1)}, bf16[12,192,384]{2,1,0:T(8,128)(2,1)}, u32[]{:S(2)}, u32[]{:S(2)}) collective-permute-start(bf16[12,192,384]{2,1,0:T(8,128)(2,1)} %get-tuple-element.485), channel_id=1, source_target_pairs={{0,4},{2,6},{4,0},{6,2},{8,12},{10,14},{12,8},{14,10},{16,20},{18,... | collective-permute-start | bytes 5308424 | tf_op jit(solution)/shard_map/ppermute | solution.py:1060
  331.7 41.0 %collective-permute-start.32 = (bf16[12,192,384]{2,1,0:T(8,128)(2,1)}, bf16[12,192,384]{2,1,0:T(8,128)(2,1)}, u32[]{:S(2)}, u32[]{:S(2)}) collective-permute-start(bf16[12,192,384]{2,1,0:T(8,128)(2,1)} %get-tuple-element.487), channel_id=1, source_target_pairs={{0,2},{2,0},{4,6},{6,4},{8,10},{10,8},{12,14},{14,12},{16,18},{18,... | collective-permute-start | bytes 5308424 | tf_op jit(solution)/shard_map/ppermute | solution.py:1056
  372.7 38.7 %collective-permute-start.37 = (bf16[6,192,384]{2,1,0:T(8,128)(2,1)}, bf16[6,192,384]{2,1,0:T(8,128)(2,1)}, u32[]{:S(2)}, u32[]{:S(2)}) collective-permute-start(bf16[6,192,384]{2,1,0:T(8,128)(2,1)} %get-tuple-element.502), channel_id=1, source_target_pairs={{0,4},{2,6},{4,0},{6,2},{8,12},{10,14},{12,8},{14,10},{16,20},{18,... | collective-permute-start | bytes 2654216 | tf_op jit(solution)/shard_map/ppermute | solution.py:1060
  374.1 37.4 %collective-permute-start.38 = (bf16[6,192,384]{2,1,0:T(8,128)(2,1)}, bf16[6,192,384]{2,1,0:T(8,128)(2,1)}, u32[]{:S(2)}, u32[]{:S(2)}) collective-permute-start(bf16[6,192,384]{2,1,0:T(8,128)(2,1)} %get-tuple-element.504), channel_id=1, source_target_pairs={{0,2},{2,0},{4,6},{6,4},{8,10},{10,8},{12,14},{14,12},{16,18},{18,... | collective-permute-start | bytes 2654216 | tf_op jit(solution)/shard_map/ppermute | solution.py:1056
  380.3 33.7 %collective-permute-start.36 = (bf16[2,3,192,384]{3,2,1,0:T(8,128)(2,1)}, bf16[2,3,192,384]{3,2,1,0:T(8,128)(2,1)}, u32[]{:S(2)}, u32[]{:S(2)}) collective-permute-start(bf16[2,3,192,384]{3,2,1,0:T(8,128)(2,1)} %get-tuple-element.654), channel_id=1, source_target_pairs={{0,4},{2,6},{4,0},{6,2},{8,12},{10,14},{12,8},{14,10},{16,20},{18,... | collective-permute-start | bytes 2654216 | tf_op jit(solution)/shard_map/ppermute | solution.py:1060
  384.4 30.7 %collective-permute-start.35 = (bf16[2,3,192,384]{3,2,1,0:T(8,128)(2,1)}, bf16[2,3,192,384]{3,2,1,0:T(8,128)(2,1)}, u32[]{:S(2)}, u32[]{:S(2)}) collective-permute-start(bf16[2,3,192,384]{3,2,1,0:T(8,128)(2,1)} %get-tuple-element.656), channel_id=1, source_target_pairs={{0,2},{2,0},{4,6},{6,4},{8,10},{10,8},{12,14},{14,12},{16,18},{18,... | collective-permute-start | bytes 2654216 | tf_op jit(solution)/shard_map/ppermute | solution.py:1056
  420.6 40.9 %collective-permute-start.39 = (bf16[6,192,384]{2,1,0:T(8,128)(2,1)}, bf16[6,192,384]{2,1,0:T(8,128)(2,1)}, u32[]{:S(2)}, u32[]{:S(2)}) collective-permute-start(bf16[6,192,384]{2,1,0:T(8,128)(2,1)} %get-tuple-element.650), channel_id=1, source_target_pairs={{24,16},{26,18},{28,20},{30,22},{25,17},{27,19},{29,21},{31,23}} | collective-permute-start | bytes 2654216 | tf_op jit(solution)/shard_map/ppermute | solution.py:1064
  424.8 35.1 %collective-permute-start.41 = (bf16[1,3,192,384]{3,2,1,0:T(8,128)(2,1)}, bf16[1,3,192,384]{3,2,1,0:T(8,128)(2,1)}, u32[]{:S(2)}, u32[]{:S(2)}) collective-permute-start(bf16[1,3,192,384]{3,2,1,0:T(8,128)(2,1)} %get-tuple-element.658), channel_id=1, source_target_pairs={{0,4},{2,6},{4,0},{6,2},{8,12},{10,14},{12,8},{14,10},{16,20},{18,... | collective-permute-start | bytes 1327112 | tf_op jit(solution)/shard_map/ppermute | solution.py:1060
  425.5 45.6 %collective-permute-start.34 = (bf16[1024,768]{1,0:T(8,128)(2,1)S(1)}, bf16[1024,768]{1,0:T(8,128)(2,1)}, u32[]{:S(2)}, u32[]{:S(2)}) collective-permute-start(bf16[1024,768]{1,0:T(8,128)(2,1)S(1)} %get-tuple-element.943.refs_4_), channel_id=1, source_target_pairs={{0,1},{1,0},{2,3},{3,2},{4,5},{5,4},{6,7},{7,6},{8,9},{9,8},{10,11... | collective-permute-start | bytes 4718600 | tf_op jit(solution)/shard_map/ppermute | solution.py:881
  428.0 33.2 %collective-permute-start.40 = (bf16[1,3,192,384]{3,2,1,0:T(8,128)(2,1)}, bf16[1,3,192,384]{3,2,1,0:T(8,128)(2,1)}, u32[]{:S(2)}, u32[]{:S(2)}) collective-permute-start(bf16[1,3,192,384]{3,2,1,0:T(8,128)(2,1)} %get-tuple-element.660), channel_id=1, source_target_pairs={{0,2},{2,0},{4,6},{6,4},{8,10},{10,8},{12,14},{14,12},{16,18},{18,... | collective-permute-start | bytes 1327112 | tf_op jit(solution)/shard_map/ppermute | solution.py:1056
  430.3 39.3 %collective-permute-start.30 = (bf16[256,768]{1,0:T(8,128)(2,1)S(1)}, bf16[256,768]{1,0:T(8,128)(2,1)}, u32[]{:S(2)}, u32[]{:S(2)}) collective-permute-start(bf16[256,768]{1,0:T(8,128)(2,1)S(1)} %copy-done.20), channel_id=1, source_target_pairs={{0,1},{1,0},{2,3},{3,2},{4,5},{5,4},{6,7},{7,6},{8,9},{9,8},{10,11... | collective-permute-start | bytes 1179656 | tf_op jit(solution)/shard_map/ppermute | solution.py:881
  459.8 37.0 %collective-permute-start.45 = (bf16[6,192,384]{2,1,0:T(8,128)(2,1)}, bf16[6,192,384]{2,1,0:T(8,128)(2,1)}, u32[]{:S(2)}, u32[]{:S(2)}) collective-permute-start(bf16[6,192,384]{2,1,0:T(8,128)(2,1)} %get-tuple-element.537), channel_id=1, source_target_pairs={{0,4},{2,6},{4,0},{6,2},{8,12},{10,14},{12,8},{14,10},{16,20},{18,... | collective-permute-start | bytes 2654216 | tf_op jit(solution)/shard_map/ppermute | solution.py:1060
  461.2 35.6 %collective-permute-start.46 = (bf16[6,192,384]{2,1,0:T(8,128)(2,1)}, bf16[6,192,384]{2,1,0:T(8,128)(2,1)}, u32[]{:S(2)}, u32[]{:S(2)}) collective-permute-start(bf16[6,192,384]{2,1,0:T(8,128)(2,1)} %get-tuple-element.539), channel_id=1, source_target_pairs={{0,2},{2,0},{4,6},{6,4},{8,10},{10,8},{12,14},{14,12},{16,18},{18,... | collective-permute-start | bytes 2654216 | tf_op jit(solution)/shard_map/ppermute | solution.py:1056
  500.7 63.6 %all-to-all-start.6 = ((bf16[16,112,384]{2,1,0:T(8,128)(2,1)}), bf16[16,112,384]{2,1,0:T(8,128)(2,1)}, u32[]{:S(2)}, u32[]{:S(2)}) async-start(bf16[16,112,384]{2,1,0:T(8,128)(2,1)} %bitcast.198), calls=%async_computation.6 | async-start | bytes 2752512 | tf_op jit(solution)/shard_map/all_to_all | solution.py:1473
  546.2 40.6 %collective-permute-start.51 = (bf16[6,192,384]{2,1,0:T(8,128)(2,1)}, bf16[6,192,384]{2,1,0:T(8,128)(2,1)}, u32[]{:S(2)}, u32[]{:S(2)}) collective-permute-start(bf16[6,192,384]{2,1,0:T(8,128)(2,1)} %get-tuple-element.662), channel_id=1, source_target_pairs={{24,16},{26,18},{28,20},{30,22},{16,8},{18,10},{20,12},{22,14},{8,... | collective-permute-start | bytes 2654216 | tf_op jit(solution)/shard_map/ppermute | solution.py:1064
  (109 other events, 1621.3 us)
where the time goes:
time: 649 us; the launch traced here: 639 us
  Pallas kernels  254 us (39%)
  waiting for transfers between devices  135 us (21%)
  starting transfers between devices  110 us (17%)
  other arithmetic  81 us (12%)
  local copies, waits for them, and re-layouts  36.5 us (6%)
  matrix products  13.1 us (2%)
  between operations  9.23 us (1%)
    pallas_call x3, Pallas kernels, attention_backward(): call(partial(attention_backward_body, seg, order, planes, bool(carry), ca...  67.3 us
    pallas_call x2, Pallas kernels, ffn_backward(): call(partial(ffn_backward_body, seg, order, sets, len(groups)), count //...  51.2 us
    ppermute x14, waiting for transfers between devices, over_y(): return lax.ppermute(value, 'blk', [(at, at ^ 2) for at in range(16)])  51 us
    pallas_call x2, Pallas kernels, ffn_forward(): call(partial(forward_ffn_body, order), count // rows, [SMEM, by_rows(rows...  37.9 us
    ppermute x14, starting transfers between devices, over_z(): lax.ppermute(value, 'blk', [(4 * a + at, 4 * b + at) for a, b in pairs fo...  35 us
    ppermute x14, waiting for transfers between devices, over_z(): lax.ppermute(value, 'blk', [(4 * a + at, 4 * b + at) for a, b in pairs fo...  29.9 us
    pallas_call x2, Pallas kernels, attention_forward(): call(partial(attention_forward_body, seg, order), blocks, [SMEM, SMEM, by...  26.3 us
    pallas_call x1, Pallas kernels, embed_backward(): call(partial(embed_backward_body, segs[:1] + segs[1:] * len(p_parts[0]),...  21.9 us
  transfers between devices with their start and end apart: 59, of which 18 were waited for; matrix products, arithmetic and copies ran while one was open for 15% of the time, Pallas kernels for 32%

commit v1 on v0

--- a/solution.py
+++ b/solution.py
@@ -297,7 +297,7 @@
     value = hat * params[1:2] + params[2:3]
     hidden[...] = value
     low = value.astype(bf16)
-    step = 2 * wide if UNITS % (2 * wide) == 0 else wide
+    step = UNITS
     result = jnp.zeros(out.shape, f32)
     for start in range(0, UNITS, step):
         columns = slice(start, start + step)
@@ -361,7 +361,7 @@
     sums[2:3, :] += total(d_output)
     low = d_sum.astype(bf16)
     hidden_low = value.astype(bf16)
-    step = 2 * wide if UNITS % (2 * wide) == 0 else wide
+    step = UNITS
     result = jnp.zeros(out.shape, f32)
     for start in range(0, UNITS, step):
         columns = slice(start, start + step)
@@ -1298,7 +1298,7 @@
         )
         far_one = far_two
         far_two = gather_far(links, *near_two)
-    halves = expand(length, place_columns, fetched.reshape(-1, half))
+    halves = expand(tall_rows(place_columns), place_columns, fetched.reshape(-1, half))
 
     def fetch_more(carry):
         done, total = carry
@@ -1341,7 +1341,7 @@
         hidden, _, _, own_two = kept[11:]
         other_two = other_core(own_two)
         kept.append(other_two)
-        return pool_forward(layer, seg, length, lengths, hidden, own_two, other_two, params)
+        return pool_forward(layer, seg, tall_rows(hidden), lengths, hidden, own_two, other_two, params)
 
     if known:
         near_one = gather_near(links, early_one)

time: 649 us -> 645 us (level)
  transfers between devices with their start and end apart: 59 -> 59, of which waited for: 18 -> 20; matrix products, arithmetic and copies ran while one was open for 15% -> 15% of each run, Pallas kernels for 32% -> 31%
where the time goes in v1:
time: 645 us; the launch traced here: 635 us
  Pallas kernels  249 us (39%)
  waiting for transfers between devices  136 us (21%)
  starting transfers between devices  110 us (17%)
  other arithmetic  81 us (13%)
  local copies, waits for them, and re-layouts  36.5 us (6%)
  matrix products  13.1 us (2%)
  between operations  9.18 us (1%)
    pallas_call x3, Pallas kernels, attention_backward(): call(partial(attention_backward_body, seg, order, planes, bool(carry), ca...  67.3 us
    ppermute x14, waiting for transfers between devices, over_y(): return lax.ppermute(value, 'blk', [(at, at ^ 2) for at in range(16)])  50.7 us
    pallas_call x2, Pallas kernels, ffn_backward(): call(partial(ffn_backward_body, seg, order, sets, len(groups)), count //...  50.2 us
    pallas_call x2, Pallas kernels, ffn_forward(): call(partial(forward_ffn_body, order), count // rows, [SMEM, by_rows(rows...  37.1 us
    ppermute x14, starting transfers between devices, over_z(): lax.ppermute(value, 'blk', [(4 * a + at, 4 * b + at) for a, b in pairs fo...  35 us
    ppermute x14, waiting for transfers between devices, over_z(): lax.ppermute(value, 'blk', [(4 * a + at, 4 * b + at) for a, b in pairs fo...  29.9 us
    pallas_call x2, Pallas kernels, attention_forward(): call(partial(attention_forward_body, seg, order), blocks, [SMEM, SMEM, by...  26.3 us
    pallas_call x1, Pallas kernels, embed_backward(): call(partial(embed_backward_body, segs[:1] + segs[1:] * len(p_parts[0]),...  21.9 us
  transfers between devices with their start and end apart: 59, of which 20 were waited for; matrix products, arithmetic and copies ran while one was open for 15% of the time, Pallas kernels for 31%

profile of v1, /device:TPU:0, one launch (start us, length us, event | category | flops | bytes accessed | tf_op | source)
XLA Modules:
  0.0 635.4 jit_solution(10376880927684598789)
XLA Ops:
  23.3 9.3 %collective-permute-done.2 = bf16[6,192,384]{2,1,0:T(8,128)(2,1)} collective-permute-done((bf16[6,192,384]{2,1,0:T(8,128)(2,1)}, bf16[6,192,384]{2,1,0:T(8,128)(2,1)}, u32[]{:S(2)}, u32[]{:S(2)}) %collective-permute-start.2) | collective-permute-done | bytes 884768 | tf_op jit(solution)/shard_map/ppermute | solution.py:1064
  32.6 7.6 %collective-permute-done.3 = bf16[6,192,384]{2,1,0:T(8,128)(2,1)} collective-permute-done((bf16[6,192,384]{2,1,0:T(8,128)(2,1)}, bf16[6,192,384]{2,1,0:T(8,128)(2,1)}, u32[]{:S(2)}, u32[]{:S(2)}) %collective-permute-start.3) | collective-permute-done | bytes 884768 | tf_op jit(solution)/shard_map/ppermute | solution.py:1064
  43.1 7.6 %all-to-all-start.2 = ((bf16[16,72,128]{2,1,0:T(8,128)(2,1)}), bf16[16,72,128]{2,1,0:T(8,128)(2,1)S(1)}, u32[]{:S(2)}, u32[]{:S(2)}) async-start(bf16[16,72,128]{2,1,0:T(8,128)(2,1)} %pad_maximum_fusion.1), calls=%async_computation.2 | async-start | bytes 589824 | tf_op jit(solution)/shard_map/all_to_all | solution.py:1221
  50.8 18.0 %all-to-all-done.2 = bf16[16,72,128]{2,1,0:T(8,128)(2,1)S(1)} async-done(((bf16[16,72,128]{2,1,0:T(8,128)(2,1)}), bf16[16,72,128]{2,1,0:T(8,128)(2,1)S(1)}, u32[]{:S(2)}, u32[]{:S(2)}) %all-to-all-start.2) | async-done | bytes 294944 | tf_op jit(solution)/shard_map/all_to_all | solution.py:1221
  92.7 9.8 %all-to-all-start.3 = ((bf16[16,112,384]{2,1,0:T(8,128)(2,1)}), bf16[16,112,384]{2,1,0:T(8,128)(2,1)}, u32[]{:S(2)}, u32[]{:S(2)}) async-start(bf16[16,112,384]{2,1,0:T(8,128)(2,1)} %maximum_maximum_fusion), calls=%async_computation.3 | async-start | bytes 2752512 | tf_op jit(solution)/shard_map/all_to_all | solution.py:1294
  111.8 33.2 %collective-permute-done.10.rest_3_ = bf16[3,192,384]{2,1,0:T(8,128)(2,1)S(1)} collective-permute-done((bf16[3,192,384]{2,1,0:T(8,128)(2,1)S(1)}, bf16[3,192,384]{2,1,0:T(8,128)(2,1)S(1)}, u32[]{:S(2)}, u32[]{:S(2)}) %collective-permute-start.10) | collective-permute-done | bytes 442400 | tf_op jit(solution)/shard_map/ppermute | solution.py:1060
  170.9 20.6 %attention_forward_1.1 = (f32[2048,768]{1,0:T(8,128)}, bf16[2048,1152]{1,0:T(8,128)(2,1)}, bf16[2048,384]{1,0:T(8,128)(2,1)}, f32[2048,128]{1,0:T(8,128)}, bf16[2048,768]{1,0:T(8,128)(2,1)}) custom-call(s32[8]{0:T(128)} %lengths.15, s32[5]{0:T(128)S(1)} %stack.31.spot.refs_22_, bf16[2560,384]{1,0:T(8,128)(2,1)S(1)} %get-tuple-element.956.mine.place_mine.refs_17_.refs_19_, ...), custom_call_target="tpu_custom_call" | custom-call | flops 2300000000 | bytes 200000 | tf_op jit(solution)/shard_map/attention_forward_1/pallas_call | solution.py:594
  200.1 29.1 %ffn_forward_1.1 = (f32[2048,768]{1,0:T(8,128)}, bf16[2048,1536]{1,0:T(8,128)(2,1)}, bf16[2048,1536]{1,0:T(8,128)(2,1)}, bf16[2048,768]{1,0:T(8,128)(2,1)}) custom-call(s32[5]{0:T(128)S(1)} %stack.31.spot.refs_22_, f32[2048,768]{1,0:T(8,128)} %get-tuple-element.442.state, bf16[2048,768]{1,0:T(8,128)(2,1)} %get-tuple-element.443.own, ...), custom_call_target="tpu_custom_call" | custom-call | flops 3496000000 | bytes 304000 | tf_op jit(solution)/shard_map/ffn_forward_1/pallas_call | solution.py:634
  236.4 8.3 %pool_1.1 = f32[8,768]{1,0:T(8,128)} custom-call(s32[8]{0:T(128)} %lengths.15, f32[2048,768]{1,0:T(8,128)} %get-tuple-element.451.hidden, bf16[2048,768]{1,0:T(8,128)(2,1)} %get-tuple-element.452.own, bf16[2048,768]{1,0:T(8,128)(2,1)} %collective-permute-done.24.other, f32[6,768]{1,0:T(8,128)} %slice.188.params), custom_call_target="tpu_custom_call" | custom-call | flops 506000000 | bytes 44000 | tf_op jit(solution)/shard_map/pool_1/pallas_call | solution.py:670
  259.9 8.0 %ffn_forward_0.1 = (f32[256,768]{1,0:T(8,128)}, bf16[256,1536]{1,0:T(8,128)(2,1)}, bf16[256,1536]{1,0:T(8,128)(2,1)}, bf16[256,768]{1,0:T(8,128)(2,1)}) custom-call(s32[5]{0:T(128)S(1)} %stack.31.spot.refs_22_, f32[256,768]{1,0:T(8,128)} %get-tuple-element.455.state, bf16[256,768]{1,0:T(8,128)(2,1)} %get-tuple-element.456.own, bf16[256,768]{1,0:T(8,128)(2,1)} %copy-done.40, ...), custom_call_target="tpu_custom_call" | custom-call | flops 437000000 | bytes 38000 | tf_op jit(solution)/shard_map/ffn_forward_0/pallas_call | solution.py:634
  282.4 12.1 %all-to-all-done.5 = f32[16,5,768]{2,1,0:T(8,128)S(1)} async-done(((f32[16,5,768]{2,1,0:T(8,128)}), f32[16,5,768]{2,1,0:T(8,128)S(1)}, u32[]{:S(2)}, u32[]{:S(2)}) %all-to-all-start.5) | async-done | bytes 245792 | tf_op jit(solution)/shard_map/all_to_all | solution.py:885
  301.7 12.1 %ffn_backward_0.1 = (f32[256,768]{1,0:T(8,128)}, bf16[256,768]{1,0:T(8,128)(2,1)}, f32[8,768]{1,0:T(8,128)}, f32[1,1536]{1,0:T(1,128)}, bf16[12,192,384]{2,1,0:T...) custom-call(s32[4]{0:T(128)} %lengths.13, ...), custom_call_target="tpu_custom_call" | custom-call | flops 552000000 | bytes 48000 | tf_op jit(solution)/shard_map/ffn_backward_0/pallas_call | solution.py:702
  316.6 11.3 %attention_backward_0_0.1 = (f32[256,768]{1,0:T(8,128)}, bf16[256,768]{1,0:T(8,128)(2,1)}, f32[8,768]{1,0:T(8,128)}, f32[1,1152]{1,0:T(1,128)}, bf16[12,192,384]...) custom-call(s32[4]{0:T(128)} %lengths.13, ...), custom_call_target="tpu_custom_call", output_to_operand_aliasing={{4}: (22, {}), {5}: (23, {}), {6}: (24, {}), {7}: (25, {})} | custom-call | flops 667000000 | bytes 58000 | tf_op jit(solution)/shard_map/attention_backward_0_0/pallas_call | solution.py:763
  330.8 38.1 %ffn_backward_1.1 = (f32[2048,768]{1,0:T(8,128)}, bf16[2048,768]{1,0:T(8,128)(2,1)}, f32[8,768]{1,0:T(8,128)}, f32[1,1536]{1,0:T(1,128)}, bf16[6,192,384]{2,1,0:...) custom-call(s32[8]{0:T(128)} %lengths.15, ...), custom_call_target="tpu_custom_call" | custom-call | flops 4416000000 | bytes 384000 | tf_op jit(solution)/shard_map/ffn_backward_1/pallas_call | solution.py:702
  381.4 26.7 %attention_backward_1_0.1 = (f32[1024,768]{1,0:T(8,128)}, bf16[1024,768]{1,0:T(8,128)(2,1)S(1)}, f32[8,768]{1,0:T(8,128)}, f32[1,1152]{1,0:T(1,128)}, f32[768,1152]{1,0:T(8,128)}, /*index=5*/f32[384,768]{1,0:T(8,128)}) custom-call(s32[8]{0:T(128)} %lengths.15, s32[5]{0:T(128)S(1)} %stack.31.spot.refs_22_, f32[2048,768]{1,0:T(8,128)} %get-tuple-element.482.carried, ...), custom_call_target="tpu_custom_call" | custom-call | flops 2668000000 | bytes 232000 | tf_op jit(solution)/shard_map/attention_backward_1_0/pallas_call | solution.py:763
  426.7 29.3 %attention_backward_1_4.1 = (f32[1024,768]{1,0:T(8,128)}, bf16[1024,768]{1,0:T(8,128)(2,1)}, f32[8,768]{1,0:T(8,128)S(1)}, f32[1,1152]{1,0:T(1,128)S(1)}, bf16[6...) custom-call(s32[4]{0:T(128)} %slice.199.lengths, ...), custom_call_target="tpu_custom_call", output_to_operand_aliasing={{4}: (26, {}), {5}: (27, {}), {6}: (28, {}), {7}: (29, {})} | custom-call | flops 2668000000 | bytes 232000 | tf_op jit(solution)/shard_map/attention_backward_1_4/pallas_call | solution.py:763
  471.6 21.9 %embed_backward.2 = (bf16[1792,384]{1,0:T(8,128)(2,1)}, f32[8,768]{1,0:T(8,128)}) custom-call(f32[256,768]{1,0:T(8,128)} %get-tuple-element.939.refs_0_, bf16[256,768]{1,0:T(8,128)(2,1)S(1)} %copy-done.20, bf16[256,768]{1,0:T(8,128)(2,1)} %collective-permute-done.30.refs_2_, f32[1024,768]{1,0:T(8,128)} %get-tuple-element.942.refs_3_, ...), custom_call_target="tpu_custom_call" | custom-call | flops 2300000000 | bytes 200000 | tf_op jit(solution)/shard_map/embed_backward/pallas_call | solution.py:837
  510.4 14.4 %collective-permute-done.48 = bf16[1,3,192,384]{3,2,1,0:T(8,128)(2,1)S(1)} collective-permute-done((bf16[1,3,192,384]{3,2,1,0:T(8,128)(2,1)S(1)}, bf16[1,3,192,384]{3,2,1,0:T(8,128)(2,1)S(1)}, u32[]{:S(2)}, u32[]{:S(2)}) %collective-permute-start.48) | collective-permute-done | bytes 442400 | tf_op jit(solution)/shard_map/ppermute | solution.py:1060
  543.8 9.0 %collective-permute-done.49 = bf16[6,192,384]{2,1,0:T(8,128)(2,1)} collective-permute-done((bf16[6,192,384]{2,1,0:T(8,128)(2,1)}, bf16[6,192,384]{2,1,0:T(8,128)(2,1)}, u32[]{:S(2)}, u32[]{:S(2)}) %collective-permute-start.49) | collective-permute-done | bytes 884768 | tf_op jit(solution)/shard_map/ppermute | solution.py:1064
  583.2 10.4 %block_products.1 = (f32[12,192,192]{2,1,0:T(8,128)}, f32[12,192,192]{2,1,0:T(8,128)}, f32[12,192,192]{2,1,0:T(8,128)}, f32[12,192,192]{2,1,0:T(8,128)}, f32[8,192]{1,0:T(8,128)}) custom-call(f32[1]{0:T(128)} %bitcast.52.inverse, f32[1,12,192,192]{3,2,1,0:T(8,128)} %left.2, f32[1,12,192,192]{3,2,1,0:T(8,128)} %right.2, ...), custom_call_target="tpu_custom_call" | custom-call | flops 1150000000 | bytes 100000 | tf_op jit(solution)/shard_map/block_products/pallas_call | solution.py:1011
  596.2 7.7 %all-to-all-start.8 = ((f32[32,8,128]{2,1,0:T(8,128)}), f32[32,8,128]{2,1,0:T(8,128)S(1)}, u32[]{:S(2)}, u32[]{:S(2)}) async-start(f32[32,8,128]{2,1,0:T(8,128)} %broadcast_in_dim.128), calls=%async_computation.8 | async-start | bytes 262144 | tf_op jit(solution)/shard_map/all_to_all | solution.py:1550
  604.1 8.1 %all-to-all-done.8 = f32[32,8,128]{2,1,0:T(8,128)S(1)} async-done(((f32[32,8,128]{2,1,0:T(8,128)}), f32[32,8,128]{2,1,0:T(8,128)S(1)}, u32[]{:S(2)}, u32[]{:S(2)}) %all-to-all-start.8) | async-done | bytes 131104 | tf_op jit(solution)/shard_map/all_to_all | solution.py:1550
  615.2 9.5 %multiply_subtract_fusion = (f32[1944,384]{1,0:T(8,128)}, f32[1944,384]{1,0:T(8,128)}, f32[1944,384]{1,0:T(8,128)}) fusion(f32[1944,384]{1,0:T(8,128)} %param.30, f32[]{:T(128)} %min.11, s32[]{:T(128)S(6)} %min.12, f32[1944,384]{1,0:T(8,128)S(1)} %broadcast_in_dim.130, f32[256,384]{1,0:T(8,128)S(1)} %bitcast.196, f32[1944,384]{1,0:T(8,128)} %get-tuple-element.541, ...), kind=kLoop, calls=%fused_computation.45 | loop fusion | flops 17915904 | bytes 24281100 | tf_op jit(solution)/shard_map/sub | solution.py:1120
  624.6 9.2 %block_update.1 = (f32[1,12,192,192]{3,2,1,0:T(8,128)}, f32[1,12,192,192]{3,2,1,0:T(8,128)}, f32[1,12,192,192]{3,2,1,0:T(8,128)}, f32[1,12,192,192]{3,2,1,0:T(8,128)}) custom-call(f32[1]{0:T(128)} %bitcast.53.factor, f32[12,192,192]{2,1,0:T(8,128)} %get-tuple-element.554.scaled, f32[12,192,192]{2,1,0:T(8,128)} %get-tuple-element.555.square, ...), custom_call_target="tpu_custom_call" | custom-call | flops 1035000000 | bytes 90000 | tf_op jit(solution)/shard_map/block_update/pallas_call | solution.py:1038
  (406 shorter events, 254.9 us)
Async XLA Ops:
  92.7 63.5 %all-to-all-start.3 = ((bf16[16,112,384]{2,1,0:T(8,128)(2,1)}), bf16[16,112,384]{2,1,0:T(8,128)(2,1)}, u32[]{:S(2)}, u32[]{:S(2)}) async-start(bf16[16,112,384]{2,1,0:T(8,128)(2,1)} %maximum_maximum_fusion), calls=%async_computation.3 | async-start | bytes 2752512 | tf_op jit(solution)/shard_map/all_to_all | solution.py:1294
  106.5 38.9 %collective-permute-start.12 = (bf16[6,192,384]{2,1,0:T(8,128)(2,1)S(1)}, bf16[6,192,384]{2,1,0:T(8,128)(2,1)}, u32[]{:S(2)}, u32[]{:S(2)}) collective-permute-start(bf16[6,192,384]{2,1,0:T(8,128)(2,1)S(1)} %select_select_fusion.4.rest_5_), channel_id=1, source_target_pairs={{0,2},{2,0},{4,6},{6,4},{8,10},{10,8},{12,14},{14,12},{16,18},{18,... | collective-permute-start | bytes 2654216 | tf_op jit(solution)/shard_map/ppermute | solution.py:1056
  108.6 36.8 %collective-permute-start.13 = (bf16[6,192,384]{2,1,0:T(8,128)(2,1)S(1)}, bf16[6,192,384]{2,1,0:T(8,128)(2,1)}, u32[]{:S(2)}, u32[]{:S(2)}) collective-permute-start(bf16[6,192,384]{2,1,0:T(8,128)(2,1)S(1)} %select_select_fusion.4.rest_5_), channel_id=1, source_target_pairs={{0,4},{2,6},{4,0},{6,2},{8,12},{10,14},{12,8},{14,10},{16,20},{18,... | collective-permute-start | bytes 2654216 | tf_op jit(solution)/shard_map/ppermute | solution.py:1060
  110.2 34.8 %collective-permute-start.10 = (bf16[3,192,384]{2,1,0:T(8,128)(2,1)S(1)}, bf16[3,192,384]{2,1,0:T(8,128)(2,1)S(1)}, u32[]{:S(2)}, u32[]{:S(2)}) collective-permute-start(bf16[3,192,384]{2,1,0:T(8,128)(2,1)S(1)} %slice.173), channel_id=1, source_target_pairs={{0,4},{2,6},{4,0},{6,2},{8,12},{10,14},{12,8},{14,10},{16,20},{18,... | collective-permute-start | bytes 1327112 | tf_op jit(solution)/shard_map/ppermute | solution.py:1060
  110.9 34.5 %collective-permute-start.11 = (bf16[3,192,384]{2,1,0:T(8,128)(2,1)S(1)}, bf16[3,192,384]{2,1,0:T(8,128)(2,1)S(1)}, u32[]{:S(2)}, u32[]{:S(2)}) collective-permute-start(bf16[3,192,384]{2,1,0:T(8,128)(2,1)S(1)} %slice.174), channel_id=1, source_target_pairs={{0,2},{2,0},{4,6},{6,4},{8,10},{10,8},{12,14},{14,12},{16,18},{18,... | collective-permute-start | bytes 1327112 | tf_op jit(solution)/shard_map/ppermute | solution.py:1056
  191.6 37.6 %collective-permute-start.22 = (bf16[6,192,384]{2,1,0:T(8,128)(2,1)S(1)}, bf16[6,192,384]{2,1,0:T(8,128)(2,1)}, u32[]{:S(2)}, u32[]{:S(2)}) collective-permute-start(bf16[6,192,384]{2,1,0:T(8,128)(2,1)S(1)} %get-tuple-element.664.rest_5_), channel_id=1, source_target_pairs={{0,2},{2,0},{4,6},{6,4},{8,10},{10,8},{12,14},{14,12},{16,18},{18,... | collective-permute-start | bytes 2654216 | tf_op jit(solution)/shard_map/ppermute | solution.py:1056
  193.4 35.8 %collective-permute-start.23 = (bf16[6,192,384]{2,1,0:T(8,128)(2,1)S(1)}, bf16[6,192,384]{2,1,0:T(8,128)(2,1)}, u32[]{:S(2)}, u32[]{:S(2)}) collective-permute-start(bf16[6,192,384]{2,1,0:T(8,128)(2,1)S(1)} %get-tuple-element.664.rest_5_), channel_id=1, source_target_pairs={{0,4},{2,6},{4,0},{6,2},{8,12},{10,14},{12,8},{14,10},{16,20},{18,... | collective-permute-start | bytes 2654216 | tf_op jit(solution)/shard_map/ppermute | solution.py:1060
  196.2 33.0 %collective-permute-start.20 = (bf16[3,192,384]{2,1,0:T(8,128)(2,1)}, bf16[3,192,384]{2,1,0:T(8,128)(2,1)S(1)}, u32[]{:S(2)}, u32[]{:S(2)}) collective-permute-start(bf16[3,192,384]{2,1,0:T(8,128)(2,1)} %slice.189), channel_id=1, source_target_pairs={{0,4},{2,6},{4,0},{6,2},{8,12},{10,14},{12,8},{14,10},{16,20},{18,... | collective-permute-start | bytes 1327112 | tf_op jit(solution)/shard_map/ppermute | solution.py:1060
  199.0 30.2 %collective-permute-start.21 = (bf16[3,192,384]{2,1,0:T(8,128)(2,1)}, bf16[3,192,384]{2,1,0:T(8,128)(2,1)}, u32[]{:S(2)}, u32[]{:S(2)}) collective-permute-start(bf16[3,192,384]{2,1,0:T(8,128)(2,1)} %slice.190), channel_id=1, source_target_pairs={{0,2},{2,0},{4,6},{6,4},{8,10},{10,8},{12,14},{14,12},{16,18},{18,... | collective-permute-start | bytes 1327112 | tf_op jit(solution)/shard_map/ppermute | solution.py:1056
  327.9 41.0 %collective-permute-start.31 = (bf16[12,192,384]{2,1,0:T(8,128)(2,1)}, bf16[12,192,384]{2,1,0:T(8,128)(2,1)}, u32[]{:S(2)}, u32[]{:S(2)}) collective-permute-start(bf16[12,192,384]{2,1,0:T(8,128)(2,1)} %get-tuple-element.485), channel_id=1, source_target_pairs={{0,4},{2,6},{4,0},{6,2},{8,12},{10,14},{12,8},{14,10},{16,20},{18,... | collective-permute-start | bytes 5308424 | tf_op jit(solution)/shard_map/ppermute | solution.py:1060
  328.8 40.7 %collective-permute-start.32 = (bf16[12,192,384]{2,1,0:T(8,128)(2,1)}, bf16[12,192,384]{2,1,0:T(8,128)(2,1)}, u32[]{:S(2)}, u32[]{:S(2)}) collective-permute-start(bf16[12,192,384]{2,1,0:T(8,128)(2,1)} %get-tuple-element.487), channel_id=1, source_target_pairs={{0,2},{2,0},{4,6},{6,4},{8,10},{10,8},{12,14},{14,12},{16,18},{18,... | collective-permute-start | bytes 5308424 | tf_op jit(solution)/shard_map/ppermute | solution.py:1056
  369.5 38.6 %collective-permute-start.37 = (bf16[6,192,384]{2,1,0:T(8,128)(2,1)}, bf16[6,192,384]{2,1,0:T(8,128)(2,1)}, u32[]{:S(2)}, u32[]{:S(2)}) collective-permute-start(bf16[6,192,384]{2,1,0:T(8,128)(2,1)} %get-tuple-element.502), channel_id=1, source_target_pairs={{0,4},{2,6},{4,0},{6,2},{8,12},{10,14},{12,8},{14,10},{16,20},{18,... | collective-permute-start | bytes 2654216 | tf_op jit(solution)/shard_map/ppermute | solution.py:1060
  370.7 37.5 %collective-permute-start.38 = (bf16[6,192,384]{2,1,0:T(8,128)(2,1)}, bf16[6,192,384]{2,1,0:T(8,128)(2,1)}, u32[]{:S(2)}, u32[]{:S(2)}) collective-permute-start(bf16[6,192,384]{2,1,0:T(8,128)(2,1)} %get-tuple-element.504), channel_id=1, source_target_pairs={{0,2},{2,0},{4,6},{6,4},{8,10},{10,8},{12,14},{14,12},{16,18},{18,... | collective-permute-start | bytes 2654216 | tf_op jit(solution)/shard_map/ppermute | solution.py:1056
  376.6 34.3 %collective-permute-start.36 = (bf16[2,3,192,384]{3,2,1,0:T(8,128)(2,1)}, bf16[2,3,192,384]{3,2,1,0:T(8,128)(2,1)}, u32[]{:S(2)}, u32[]{:S(2)}) collective-permute-start(bf16[2,3,192,384]{3,2,1,0:T(8,128)(2,1)} %get-tuple-element.654), channel_id=1, source_target_pairs={{0,4},{2,6},{4,0},{6,2},{8,12},{10,14},{12,8},{14,10},{16,20},{18,... | collective-permute-start | bytes 2654216 | tf_op jit(solution)/shard_map/ppermute | solution.py:1060
  380.6 31.1 %collective-permute-start.35 = (bf16[2,3,192,384]{3,2,1,0:T(8,128)(2,1)}, bf16[2,3,192,384]{3,2,1,0:T(8,128)(2,1)}, u32[]{:S(2)}, u32[]{:S(2)}) collective-permute-start(bf16[2,3,192,384]{3,2,1,0:T(8,128)(2,1)} %get-tuple-element.656), channel_id=1, source_target_pairs={{0,2},{2,0},{4,6},{6,4},{8,10},{10,8},{12,14},{14,12},{16,18},{18,... | collective-permute-start | bytes 2654216 | tf_op jit(solution)/shard_map/ppermute | solution.py:1056
  417.2 40.9 %collective-permute-start.39 = (bf16[6,192,384]{2,1,0:T(8,128)(2,1)}, bf16[6,192,384]{2,1,0:T(8,128)(2,1)}, u32[]{:S(2)}, u32[]{:S(2)}) collective-permute-start(bf16[6,192,384]{2,1,0:T(8,128)(2,1)} %get-tuple-element.650), channel_id=1, source_target_pairs={{24,16},{26,18},{28,20},{30,22},{25,17},{27,19},{29,21},{31,23}} | collective-permute-start | bytes 2654216 | tf_op jit(solution)/shard_map/ppermute | solution.py:1064
  421.4 34.6 %collective-permute-start.41 = (bf16[1,3,192,384]{3,2,1,0:T(8,128)(2,1)}, bf16[1,3,192,384]{3,2,1,0:T(8,128)(2,1)}, u32[]{:S(2)}, u32[]{:S(2)}) collective-permute-start(bf16[1,3,192,384]{3,2,1,0:T(8,128)(2,1)} %get-tuple-element.658), channel_id=1, source_target_pairs={{0,4},{2,6},{4,0},{6,2},{8,12},{10,14},{12,8},{14,10},{16,20},{18,... | collective-permute-start | bytes 1327112 | tf_op jit(solution)/shard_map/ppermute | solution.py:1060
  422.3 45.5 %collective-permute-start.34 = (bf16[1024,768]{1,0:T(8,128)(2,1)S(1)}, bf16[1024,768]{1,0:T(8,128)(2,1)}, u32[]{:S(2)}, u32[]{:S(2)}) collective-permute-start(bf16[1024,768]{1,0:T(8,128)(2,1)S(1)} %get-tuple-element.943.refs_4_), channel_id=1, source_target_pairs={{0,1},{1,0},{2,3},{3,2},{4,5},{5,4},{6,7},{7,6},{8,9},{9,8},{10,11... | collective-permute-start | bytes 4718600 | tf_op jit(solution)/shard_map/ppermute | solution.py:881
  424.8 32.6 %collective-permute-start.40 = (bf16[1,3,192,384]{3,2,1,0:T(8,128)(2,1)}, bf16[1,3,192,384]{3,2,1,0:T(8,128)(2,1)}, u32[]{:S(2)}, u32[]{:S(2)}) collective-permute-start(bf16[1,3,192,384]{3,2,1,0:T(8,128)(2,1)} %get-tuple-element.660), channel_id=1, source_target_pairs={{0,2},{2,0},{4,6},{6,4},{8,10},{10,8},{12,14},{14,12},{16,18},{18,... | collective-permute-start | bytes 1327112 | tf_op jit(solution)/shard_map/ppermute | solution.py:1056
  426.5 39.7 %collective-permute-start.30 = (bf16[256,768]{1,0:T(8,128)(2,1)S(1)}, bf16[256,768]{1,0:T(8,128)(2,1)}, u32[]{:S(2)}, u32[]{:S(2)}) collective-permute-start(bf16[256,768]{1,0:T(8,128)(2,1)S(1)} %copy-done.20), channel_id=1, source_target_pairs={{0,1},{1,0},{2,3},{3,2},{4,5},{5,4},{6,7},{7,6},{8,9},{9,8},{10,11... | collective-permute-start | bytes 1179656 | tf_op jit(solution)/shard_map/ppermute | solution.py:881
  456.1 37.4 %collective-permute-start.45 = (bf16[6,192,384]{2,1,0:T(8,128)(2,1)}, bf16[6,192,384]{2,1,0:T(8,128)(2,1)}, u32[]{:S(2)}, u32[]{:S(2)}) collective-permute-start(bf16[6,192,384]{2,1,0:T(8,128)(2,1)} %get-tuple-element.537), channel_id=1, source_target_pairs={{0,4},{2,6},{4,0},{6,2},{8,12},{10,14},{12,8},{14,10},{16,20},{18,... | collective-permute-start | bytes 2654216 | tf_op jit(solution)/shard_map/ppermute | solution.py:1060
  457.4 36.0 %collective-permute-start.46 = (bf16[6,192,384]{2,1,0:T(8,128)(2,1)}, bf16[6,192,384]{2,1,0:T(8,128)(2,1)}, u32[]{:S(2)}, u32[]{:S(2)}) collective-permute-start(bf16[6,192,384]{2,1,0:T(8,128)(2,1)} %get-tuple-element.539), channel_id=1, source_target_pairs={{0,2},{2,0},{4,6},{6,4},{8,10},{10,8},{12,14},{14,12},{16,18},{18,... | collective-permute-start | bytes 2654216 | tf_op jit(solution)/shard_map/ppermute | solution.py:1056
  496.9 63.6 %all-to-all-start.6 = ((bf16[16,112,384]{2,1,0:T(8,128)(2,1)}), bf16[16,112,384]{2,1,0:T(8,128)(2,1)}, u32[]{:S(2)}, u32[]{:S(2)}) async-start(bf16[16,112,384]{2,1,0:T(8,128)(2,1)} %bitcast.198), calls=%async_computation.6 | async-start | bytes 2752512 | tf_op jit(solution)/shard_map/all_to_all | solution.py:1473
  542.5 40.6 %collective-permute-start.51 = (bf16[6,192,384]{2,1,0:T(8,128)(2,1)}, bf16[6,192,384]{2,1,0:T(8,128)(2,1)}, u32[]{:S(2)}, u32[]{:S(2)}) collective-permute-start(bf16[6,192,384]{2,1,0:T(8,128)(2,1)} %get-tuple-element.662), channel_id=1, source_target_pairs={{24,16},{26,18},{28,20},{30,22},{16,8},{18,10},{20,12},{22,14},{8,... | collective-permute-start | bytes 2654216 | tf_op jit(solution)/shard_map/ppermute | solution.py:1064
  (109 other events, 1612.8 us)
